TPU v7x, 128 devices: a whole 4x4x4 slice. The times are simulated.
128 devices in a mesh: dp: 4 (over x), row: 2 (over core), col: 16 (over z, y).
Axes of the slice: x: 4, y: 4, z: 4, core: 2. Of those that a mesh axis runs over, the one named last changes fastest.
Arguments:
- hidden_in: bfloat16 [8192, 1024], P(('dp', 'col'), 'row'), may hold values from -6 to 6
- segment_ids: int32 [4, 2048], P('dp'), may hold values from 0 to 3, never falling along the last dimension, each value on 1 to 1024 neighbouring positions
- first_gain: float32 [1024], P('row'), may hold values from 0.25 to 1.75
- mixer_b: bfloat16 [1024, 1024], P('row', 'col'), may hold values from -0.1875 to 0.1875
- mixer_c: bfloat16 [1024, 1024], P('row', 'col'), may hold values from -0.1875 to 0.1875
- mixer_v: bfloat16 [1024, 1024], P('row', 'col'), may hold values from -0.1875 to 0.1875
- conv_kernel: float32 [3, 1024], P(None, 'col'), may hold values from -3 to 3
- mixer_out: bfloat16 [1024, 1024], P('col', 'row'), may hold values from -0.1875 to 0.1875
- second_gain: float32 [1024], P('row'), may hold values from 0.25 to 1.75
- gate_weight: bfloat16 [1024, 4608], P('row', 'col'), may hold values from -0.1875 to 0.1875
- up_weight: bfloat16 [1024, 4608], P('row', 'col'), may hold values from -0.1875 to 0.1875
- down_weight: bfloat16 [4608, 1024], P('col', 'row'), may hold values from -0.09375 to 0.09375
- cotangent: bfloat16 [8192, 1024], P(('dp', 'col'), 'row'), may hold values from -6 to 6
Outputs:
- block_out: bfloat16 [8192, 1024], P(('dp', 'col'), 'row')
- input_grad: float32 [8192, 1024], P(('dp', 'col'), 'row')
- first_gain_grad: float32 [1024], P('row')
- mixer_b_grad: float32 [1024, 1024], P('row', 'col')
- mixer_c_grad: float32 [1024, 1024], P('row', 'col')
- mixer_v_grad: float32 [1024, 1024], P('row', 'col')
- kernel_grad: float32 [3, 1024], P(None, ('col', 'row'))
- mixer_out_grad: float32 [1024, 1024], P('col', 'row')
- second_gain_grad: float32 [1024], P('row')
- gate_grad: float32 [1024, 4608], P('row', 'col')
- up_grad: float32 [1024, 4608], P('row', 'col')
- down_grad: float32 [4608, 1024], P('col', 'row')
Inputs may be any that keep to these rules, and one draw needn't show every extreme that they name: `segment_ids`: within each sequence the ids never fall; each of the 4 documents of a sequence has 1 to 1024 tokens, and one has exactly that many.
All inputs are finite; a program needn't handle non-finite values.
Results may differ from a plain program's by a relative error of at most 0.0096.
Values may be sent and summed in bfloat16 or wider, within the bound.
A program may use at most 128 MiB of HBM per device.

v0:
```python
import jax
import jax.numpy as jnp
from jax import lax
from jax.sharding import PartitionSpec as P

EPSILON = 1e-05


def delayed(values, offset):
    if offset == 0:
        return values
    filler = jnp.zeros((values.shape[0], offset, values.shape[2]), values.dtype)
    return jnp.concatenate([filler, values[:, :-offset]], 1)


def advanced(values, offset):
    if offset == 0:
        return values
    filler = jnp.zeros((values.shape[0], offset, values.shape[2]), values.dtype)
    return jnp.concatenate([values[:, offset:], filler], 1)


def boundary(segment_ids, offset):
    sequences, length = segment_ids.shape
    prior = jnp.concatenate(
        [jnp.full((sequences, offset), -1, jnp.int32), segment_ids[:, : length - offset]], 1
    )
    return (prior == segment_ids).astype(jnp.float32)[:, :, None]


def feature_total(values):
    return lax.psum(jnp.sum(values, axis=1, keepdims=True), "row")


def gather_tokens(values):
    return lax.all_gather(values, "col", axis=0, tiled=True)


def token_total(partial_sum):
    return lax.psum_scatter(partial_sum, "col", scatter_dimension=0, tiled=True)


def channel_total(partial_sum):
    return lax.psum_scatter(partial_sum, "row", scatter_dimension=2, tiled=True)


def channel_back(shares):
    return lax.all_gather(shares, "row", axis=2, tiled=True)


def own_channels(values):
    channels = values.shape[1] // lax.axis_size("row")
    return lax.dynamic_slice_in_dim(values, lax.axis_index("row") * channels, channels, 1)


def shards(
    hidden_in,
    segment_ids,
    first_gain,
    mixer_b,
    mixer_c,
    mixer_v,
    conv_kernel,
    mixer_out,
    second_gain,
    gate_weight,
    up_weight,
    down_weight,
    cotangent,
):
    f32 = jnp.float32
    bf16 = jnp.bfloat16
    features = hidden_in.shape[1] * lax.axis_size("row")
    sequences, length = segment_ids.shape
    taps = conv_kernel.shape[0]
    x_float = hidden_in.astype(f32)
    first_scale = lax.rsqrt(feature_total(x_float * x_float) / features + EPSILON)
    first_normed = (x_float * first_scale * first_gain).astype(bf16)
    first_gathered = gather_tokens(first_normed)
    mixer_stack = jnp.stack([mixer_b, mixer_c, mixer_v], 0)
    projected = channel_total(
        jnp.einsum("td,kdc->ktc", first_gathered, mixer_stack, preferred_element_type=f32)
    )
    in_gate = projected[0]
    out_gate = projected[1]
    values = projected[2]
    channels = in_gate.shape[1]
    kernel = own_channels(conv_kernel)
    masks = [boundary(segment_ids, offset) for offset in range(taps)]
    gated_in = (in_gate * values).reshape(sequences, length, channels)
    convolved = jnp.zeros_like(gated_in)
    for offset in range(taps):
        convolved = convolved + kernel[offset][None, None, :] * masks[offset] * delayed(
            gated_in, offset
        )
    convolved = convolved.reshape(-1, channels)
    mixed = (out_gate * convolved).astype(bf16)
    mixed_gathered = channel_back(mixed[None])[0]
    residual = x_float + token_total(jnp.dot(mixed_gathered, mixer_out, preferred_element_type=f32))
    second_scale = lax.rsqrt(feature_total(residual * residual) / features + EPSILON)
    second_normed = (residual * second_scale * second_gain).astype(bf16)
    second_gathered = gather_tokens(second_normed)
    feed_stack = jnp.stack([gate_weight, up_weight], 0)
    feed_pre = channel_total(
        jnp.einsum("td,kdf->ktf", second_gathered, feed_stack, preferred_element_type=f32)
    )
    gate_pre = feed_pre[0]
    up_pre = feed_pre[1]
    sigmoid_gate = jax.nn.sigmoid(gate_pre)
    silu_gate = gate_pre * sigmoid_gate
    hidden = (silu_gate * up_pre).astype(bf16)
    hidden_gathered = channel_back(hidden[None])[0]
    block_out = (
        residual + token_total(jnp.dot(hidden_gathered, down_weight, preferred_element_type=f32))
    ).astype(bf16)
    cot_gathered = gather_tokens(cotangent)
    down_grad = jnp.einsum("tf,td->fd", hidden_gathered, cot_gathered, preferred_element_type=f32)
    hidden_part = jnp.einsum("td,fd->tf", cot_gathered, down_weight, preferred_element_type=f32)
    hidden_grad = channel_total(hidden_part[None])[0]
    gate_delta = (
        hidden_grad * up_pre * sigmoid_gate * (1.0 + gate_pre * (1.0 - sigmoid_gate))
    ).astype(bf16)
    up_delta = (hidden_grad * silu_gate).astype(bf16)
    feed_delta = channel_back(jnp.stack([gate_delta, up_delta], 0))
    gate_grad = jnp.einsum("td,tf->df", second_gathered, feed_delta[0], preferred_element_type=f32)
    up_grad = jnp.einsum("td,tf->df", second_gathered, feed_delta[1], preferred_element_type=f32)
    second_grad = token_total(
        jnp.einsum("ktf,kdf->td", feed_delta, feed_stack, preferred_element_type=f32)
    )
    second_gain_part = jnp.sum(second_grad * residual * second_scale, axis=0)
    second_weighted = second_grad * second_gain
    cube_two = second_scale * second_scale * second_scale
    residual_grad = (
        cotangent.astype(f32)
        + second_scale * second_weighted
        - residual * cube_two * (feature_total(second_weighted * residual) / features)
    )
    residual_half = residual_grad.astype(bf16)
    residual_gathered = gather_tokens(residual_half)
    mixer_out_grad = jnp.einsum(
        "tc,td->cd", mixed_gathered, residual_gathered, preferred_element_type=f32
    )
    mixed_part = jnp.einsum("td,cd->tc", residual_gathered, mixer_out, preferred_element_type=f32)
    mixed_grad = channel_total(mixed_part[None])[0]
    out_gate_delta = (mixed_grad * convolved).astype(bf16)
    conv_grad = (mixed_grad * out_gate).reshape(sequences, length, channels)
    kernel_rows = []
    gated_grad = jnp.zeros_like(conv_grad)
    for offset in range(taps):
        weighted = conv_grad * masks[offset]
        kernel_rows.append(jnp.sum(weighted * delayed(gated_in, offset), axis=(0, 1)))
        gated_grad = gated_grad + advanced(weighted, offset) * kernel[offset][None, None, :]
    kernel_full = jnp.stack(kernel_rows, 0)
    kernel_grad = kernel_full
    gated_grad = gated_grad.reshape(-1, channels)
    in_gate_delta = (gated_grad * values).astype(bf16)
    values_delta = (gated_grad * in_gate).astype(bf16)
    mixer_delta = channel_back(jnp.stack([in_gate_delta, out_gate_delta, values_delta], 0))
    mixer_b_grad = jnp.einsum(
        "td,tc->dc", first_gathered, mixer_delta[0], preferred_element_type=f32
    )
    mixer_c_grad = jnp.einsum(
        "td,tc->dc", first_gathered, mixer_delta[1], preferred_element_type=f32
    )
    mixer_v_grad = jnp.einsum(
        "td,tc->dc", first_gathered, mixer_delta[2], preferred_element_type=f32
    )
    first_grad = token_total(
        jnp.einsum("ktc,kdc->td", mixer_delta, mixer_stack, preferred_element_type=f32)
    )
    first_gain_part = jnp.sum(first_grad * x_float * first_scale, axis=0)
    first_weighted = first_grad * first_gain
    cube_one = first_scale * first_scale * first_scale
    input_grad = (
        residual_grad
        + first_scale * first_weighted
        - x_float * cube_one * (feature_total(first_weighted * x_float) / features)
    )
    first_gain_grad, second_gain_grad = lax.psum((first_gain_part, second_gain_part), "col")
    (
        first_gain_grad,
        mixer_b_grad,
        mixer_c_grad,
        mixer_v_grad,
        kernel_grad,
        mixer_out_grad,
        second_gain_grad,
        gate_grad,
        up_grad,
        down_grad,
    ) = lax.psum(
        (
            first_gain_grad,
            mixer_b_grad,
            mixer_c_grad,
            mixer_v_grad,
            kernel_grad,
            mixer_out_grad,
            second_gain_grad,
            gate_grad,
            up_grad,
            down_grad,
        ),
        "dp",
    )
    return (
        block_out,
        input_grad,
        first_gain_grad,
        mixer_b_grad,
        mixer_c_grad,
        mixer_v_grad,
        kernel_grad,
        mixer_out_grad,
        second_gain_grad,
        gate_grad,
        up_grad,
        down_grad,
    )


def solution(mesh):
    return jax.shard_map(
        shards,
        mesh=mesh,
        in_specs=(
            P(("dp", "col"), "row"),
            P("dp", None),
            P("row"),
            P("row", "col"),
            P("row", "col"),
            P("row", "col"),
            P(None, "col"),
            P("col", "row"),
            P("row"),
            P("row", "col"),
            P("row", "col"),
            P("col", "row"),
            P(("dp", "col"), "row"),
        ),
        out_specs=(
            P(("dp", "col"), "row"),
            P(("dp", "col"), "row"),
            P("row"),
            P("row", "col"),
            P("row", "col"),
            P("row", "col"),
            P(None, ("col", "row")),
            P("col", "row"),
            P("row"),
            P("row", "col"),
            P("row", "col"),
            P("col", "row"),
        ),
        check_vma=False,
    )
```

profile of v0, /device:TPU:0, one launch (start us, length us, event | category | flops | bytes accessed | tf_op | source)
XLA Modules:
  0.0 717.5 jit_solution(1481168445191105319)
XLA Ops:
  7.2 1.0 fusion.9
  8.3 2.5 psum.112
  10.8 1.7 fusion.11
  12.5 47.9 %all-gather.7.cloned.1.call-done = bf16[2048,512]{1,0:T(8,128)(2,1)} async-done(((bf16[128,512]{1,0:T(8,128)(2,1)}), bf16[2048,512]{1,0:T(8,128)(2,1)}) %all-gather.7.cloned.1.call-update) | async-done | bytes 2097168 | tf_op jit(solution)/shard_map/all_gather | solution.py:36
  60.4 3.7 convolution_bitcast_fusion.4
  64.4 10.8 %reduce-scatter.9.cloned.1.call-done = f32[3,2048,32]{1,2,0:T(8,128)} async-done(((f32[3,2048,64]{1,2,0:T(8,128)}), f32[3,2048,32]{1,2,0:T(8,128)}) %reduce-scatter.9.cloned.1.call-update) | async-done | bytes 786448 | tf_op jit(solution)/shard_map/reduce_scatter | solution.py:44
  75.2 1.1 slice_multiply_fusion
  76.2 1.3 multiply_convert_fusion.7
  77.6 2.0 all_gather.25
  79.6 0.7 copy-done.6
  80.3 2.7 fusion.22
  83.0 0.5 all-gather.13.cloned.1.call-update
  83.6 78.9 %reduce-scatter.11.cloned.1.call-done = f32[128,512]{1,0:T(8,128)} async-done(((f32[2048,512]{1,0:T(8,128)}), f32[128,512]{1,0:T(8,128)}) %reduce-scatter.11.cloned.1.call-update) | async-done | bytes 262160 | tf_op jit(solution)/shard_map/reduce_scatter | solution.py:40
  162.5 1.1 multiply_reduce_fusion.5
  163.5 2.5 psum.113
  166.0 0.8 multiply_convert_fusion.6
  166.8 42.2 %all-gather.13.cloned.1.call-done = bf16[2048,512]{1,0:T(8,128)(2,1)} async-done(((bf16[128,512]{1,0:T(8,128)(2,1)}), bf16[2048,512]{1,0:T(8,128)(2,1)}) %all-gather.13.cloned.1.call-update) | async-done | bytes 2097168 | tf_op jit(solution)/shard_map/all_gather | solution.py:36
  209.0 3.9 convolution_bitcast_fusion.3
  213.0 43.2 %all-gather.9.cloned.1.call-done = bf16[2048,512]{1,0:T(8,128)(2,1)} async-done(((bf16[128,512]{1,0:T(8,128)(2,1)}), bf16[2048,512]{1,0:T(8,128)(2,1)}) %all-gather.9.cloned.1.call-update) | async-done | bytes 2097168 | tf_op jit(solution)/shard_map/all_gather | solution.py:36
  256.1 5.1 convolution_bitcast_fusion
  261.3 8.8 %reduce-scatter.17.cloned.1.call-done = f32[1,2048,144]{1,2,0:T(8,128)} async-done(((f32[1,2048,288]{1,2,0:T(8,128)}), f32[1,2048,144]{1,2,0:T(8,128)}) %reduce-scatter.17.cloned.1.call-update) | async-done | bytes 1179664 | tf_op jit(solution)/shard_map/reduce_scatter | solution.py:44
  270.1 19.3 %reduce-scatter.13.cloned.1.call-done = f32[2,2048,144]{1,2,0:T(8,128)} async-done(((f32[2,2048,288]{1,2,0:T(8,128)}), f32[2,2048,144]{1,2,0:T(8,128)}) %reduce-scatter.13.cloned.1.call-update) | async-done | bytes 2359312 | tf_op jit(solution)/shard_map/reduce_scatter | solution.py:44
  289.4 3.6 multiply_convert_fusion.1
  292.9 1.1 pad_maximum_fusion
  294.2 0.7 all-gather.11.cloned.1.call-update
  294.9 14.4 %all-gather.15.cloned.1.call-done = bf16[2,2048,288]{1,2,0:T(8,128)(2,1)} async-done(((bf16[2,2048,144]{1,2,0:T(8,128)(2,1)}), bf16[2,2048,288]{1,2,0:T(8,128)(2,1)}) %all-gather.15.cloned.1.call-update) | async-done | bytes 2359312 | tf_op jit(solution)/shard_map/all_gather | solution.py:48
  309.3 5.5 convolution_bitcast_fusion.1
  314.8 10.0 %all-gather.11.cloned.1.call-done = bf16[1,2048,288]{1,2,0:T(8,128)(2,1)} async-done(((bf16[1,2048,144]{1,2,0:T(8,128)(2,1)}), bf16[1,2048,288]{1,2,0:T(8,128)(2,1)}) %all-gather.11.cloned.1.call-update) | async-done | bytes 1179664 | tf_op jit(solution)/shard_map/all_gather | solution.py:48
  324.8 4.5 fusion.6
  329.4 77.8 %reduce-scatter.19.cloned.1.call-done = f32[128,512]{1,0:T(8,128)} async-done(((f32[2048,512]{1,0:T(8,128)}), f32[128,512]{1,0:T(8,128)}) %reduce-scatter.19.cloned.1.call-update) | async-done | bytes 262160 | tf_op jit(solution)/shard_map/reduce_scatter | solution.py:40
  407.2 1.1 multiply_reduce_fusion
  408.3 2.5 psum.114
  410.8 77.2 %reduce-scatter.15.cloned.1.call-done = f32[128,512]{1,0:T(8,128)} async-done(((f32[2048,512]{1,0:T(8,128)}), f32[128,512]{1,0:T(8,128)}) %reduce-scatter.15.cloned.1.call-update) | async-done | bytes 262160 | tf_op jit(solution)/shard_map/reduce_scatter | solution.py:40
  488.0 2.0 fusion.32
  490.1 45.0 %all-gather.17.cloned.1.call-done = bf16[2048,512]{1,0:T(8,128)(2,1)} async-done(((bf16[128,512]{1,0:T(8,128)(2,1)}), bf16[2048,512]{1,0:T(8,128)(2,1)}) %all-gather.17.cloned.1.call-update) | async-done | bytes 2097168 | tf_op jit(solution)/shard_map/all_gather | solution.py:36
  535.1 3.1 convolution_bitcast_fusion.5
  538.3 9.8 %reduce-scatter.21.cloned.1.call-done = f32[1,2048,32]{1,2,0:T(8,128)} async-done(((f32[1,2048,64]{1,2,0:T(8,128)}), f32[1,2048,32]{1,2,0:T(8,128)}) %reduce-scatter.21.cloned.1.call-update) | async-done | bytes 262160 | tf_op jit(solution)/shard_map/reduce_scatter | solution.py:44
  548.1 1.1 multiply_reduce_fusion.3
  549.3 0.3 multiply_reduce_fusion.2
  550.1 2.5 all_gather.31
  552.6 2.7 convolution_bitcast_fusion.2
  555.5 1.3 copy-done.4
  556.9 3.0 fusion.4
  559.9 1.6 fusion.2
  561.5 1.6 fusion.3
  563.1 1.1 fusion.20
  564.2 0.5 copy-done.1
  564.7 1.1 fusion.17
  565.9 1.1 fusion.18
  567.0 1.1 fusion.19
  568.2 66.5 %reduce-scatter.23.cloned.1.call-done = f32[128,512]{1,0:T(8,128)} async-done(((f32[2048,512]{1,0:T(8,128)}), f32[128,512]{1,0:T(8,128)}) %reduce-scatter.23.cloned.1.call-update) | async-done | bytes 262160 | tf_op jit(solution)/shard_map/reduce_scatter | solution.py:40
  634.7 1.1 fusion.16
  635.8 2.5 psum.115
  638.2 38.2 %all-reduce.5 = (f32[512]{0:T(512)S(1)}, f32[512]{0:T(512)S(1)}) all-reduce(f32[512]{0:T(512)S(1)} %get-tuple-element.14, f32[512]{0:T(512)S(1)} %get-tuple-element.12), channel_id=1, replica_groups=mesh['dp'=4,'row'=2,'col'=16] {'col'}, use_global_device_ids=true, to_apply=%region_17.0 | all-reduce | flops 1024 | bytes 8192 | tf_op jit(solution)/shard_map/psum | solution.py:179
  676.4 11.4 %all-reduce.6 = (f32[512]{0:T(512)}, f32[3,32]{1,0:T(4,128)}, f32[512]{0:T(512)}) all-reduce(f32[512]{0:T(512)S(1)} %get-tuple-element.16, f32[3,32]{1,0:T(4,128)S(1)} %pad_maximum_fusion.8, f32[512]{0:T(512)S(1)} %get-tuple-element.17), channel_id=1, replica_groups=mesh['dp'=4,'row'=2,'col'=16] {'dp'}, use_global_device_ids=true, to_apply=%region_18.0 | all-reduce | flops 1120 | bytes 8960 | tf_op jit(solution)/shard_map/psum | solution.py:191
  687.7 1.8 fusion.13
  689.5 11.5 %all-reduce.10.cloned.1.call-done = (f32[512,64]{0,1:T(8,128)}, f32[512,64]{0,1:T(8,128)}, f32[512,64]{0,1:T(8,128)}, f32[64,512]{1,0:T(8,128)}, f32[512,288]{0,...) async-done(((f32[512,64]{0,1:T(8,128)}, f32[512,64]{0,1:T(8,128)}, f32[512,64]{0,1:T(8,128)}, f32[64,512]{1,0:T(8,128)}, f32[512,288]{0,1:T(8,128)}, ...) | async-done | bytes 2293776 | tf_op jit(solution)/shard_map/psum | solution.py:191
  701.0 1.7 copy.32
  702.7 1.6 copy.33
  704.3 1.6 copy.34
  705.8 1.6 copy.35
  707.4 1.9 copy.36
  709.3 0.8 copy.37
  710.1 0.8 copy.38
  (86 shorter events, 1.8 us)
Async XLA Ops:
  7.2 201.8 %copy-start = (bf16[288,512]{1,0:T(8,128)(2,1)S(1)}, bf16[288,512]{1,0:T(8,128)(2,1)}, u32[]{:S(2)}) copy-start(bf16[288,512]{1,0:T(8,128)(2,1)} %param.24) | copy-start | bytes 884740
  7.2 53.2 %all-gather.7.cloned.1.call-start = ((), (), s32[]{:S(2)}) async-start(), calls=%async_computation.8 | async-start | bytes 2228224 | tf_op jit(solution)/shard_map/all_gather | solution.py:36
  12.5 62.7 %reduce-scatter.9.cloned.1.call-start = ((), (), s32[]{:S(2)}) async-start(), calls=%async_computation.9 | async-start | bytes 2359296 | tf_op jit(solution)/shard_map/reduce_scatter | solution.py:44
  60.4 3.8 copy-start.22
  60.4 3.9 copy-start.16
  64.1 16.1 %copy-start.15 = (bf16[64,512]{1,0:T(8,128)(2,1)S(1)}, bf16[64,512]{1,0:T(8,128)(2,1)}, u32[]{:S(2)}) copy-start(bf16[64,512]{1,0:T(8,128)(2,1)} %param.20) | copy-start | bytes 196612
  64.2 98.3 %reduce-scatter.11.cloned.1.call-start = ((), (), s32[]{:S(2)}) async-start(), calls=%async_computation.10 | async-start | bytes 4456448 | tf_op jit(solution)/shard_map/reduce_scatter | solution.py:40
  79.6 0.7 copy-start.6
  83.0 79.5 %copy-start.5 = (bf16[128,512]{1,0:T(8,128)(2,1)S(1)}, bf16[128,512]{1,0:T(8,128)(2,1)}, u32[]{:S(2)}) copy-start(bf16[128,512]{1,0:T(8,128)(2,1)} %param.13) | copy-start | bytes 393220
  83.0 83.1 %copy-start.20 = (f32[512]{0:T(512)S(1)}, f32[512]{0:T(512)}, u32[]{:S(2)}) copy-start(f32[512]{0:T(512)} %param.21) | copy-start | bytes 6148
  83.0 126.0 %all-gather.13.cloned.1.call-start = ((), (), s32[]{:S(2)}) async-start(), calls=%async_computation.15 | async-start | bytes 2228224 | tf_op jit(solution)/shard_map/all_gather | solution.py:36
  83.6 172.6 %all-gather.9.cloned.1.call-start = ((), (), s32[]{:S(2)}) async-start(), calls=%async_computation.11 | async-start | bytes 2228224 | tf_op jit(solution)/shard_map/all_gather | solution.py:36
  166.8 103.3 %reduce-scatter.17.cloned.1.call-start = ((), (), s32[]{:S(2)}) async-start(), calls=%async_computation.16 | async-start | bytes 3538944 | tf_op jit(solution)/shard_map/reduce_scatter | solution.py:44
  212.9 43.2 %copy-start.13 = (bf16[512,288]{0,1:T(8,128)(2,1)S(1)}, bf16[512,288]{0,1:T(8,128)(2,1)}, u32[]{:S(2)}) copy-start(bf16[512,288]{0,1:T(8,128)(2,1)} %param.23) | copy-start | bytes 884740
  212.9 43.2 %copy-start.14 = (bf16[512,288]{0,1:T(8,128)(2,1)S(1)}, bf16[512,288]{0,1:T(8,128)(2,1)}, u32[]{:S(2)}) copy-start(bf16[512,288]{0,1:T(8,128)(2,1)} %param.22) | copy-start | bytes 884740
  212.9 76.5 %reduce-scatter.13.cloned.1.call-start = ((), (), s32[]{:S(2)}) async-start(), calls=%async_computation.12 | async-start | bytes 7077888 | tf_op jit(solution)/shard_map/reduce_scatter | solution.py:44
  261.3 48.0 %all-gather.15.cloned.1.call-start = ((), (), s32[]{:S(2)}) async-start(), calls=%async_computation.17 | async-start | bytes 3538944 | tf_op jit(solution)/shard_map/all_gather | solution.py:48
  294.1 30.7 %all-gather.11.cloned.1.call-start = ((), (), s32[]{:S(2)}) async-start(), calls=%async_computation.13 | async-start | bytes 1769472 | tf_op jit(solution)/shard_map/all_gather | solution.py:48
  294.8 112.4 %reduce-scatter.19.cloned.1.call-start = ((), (), s32[]{:S(2)}) async-start(), calls=%async_computation.18 | async-start | bytes 4456448 | tf_op jit(solution)/shard_map/reduce_scatter | solution.py:40
  314.8 173.2 %reduce-scatter.15.cloned.1.call-start = ((), (), s32[]{:S(2)}) async-start(), calls=%async_computation.14 | async-start | bytes 4456448 | tf_op jit(solution)/shard_map/reduce_scatter | solution.py:40
  329.4 158.6 %copy-start.12 = (bf16[128,512]{1,0:T(8,128)(2,1)S(1)}, bf16[128,512]{1,0:T(8,128)(2,1)}, u32[]{:S(2)}) copy-start(bf16[128,512]{1,0:T(8,128)(2,1)} %param.25) | copy-start | bytes 393220
  329.4 205.7 %all-gather.17.cloned.1.call-start = ((), (), s32[]{:S(2)}) async-start(), calls=%async_computation.19 | async-start | bytes 2228224 | tf_op jit(solution)/shard_map/all_gather | solution.py:36
  488.0 60.1 %copy-start.2 = (f32[3,2048,32]{1,2,0:T(8,128)S(1)}, f32[3,2048,32]{1,2,0:T(8,128)}, u32[]{:S(2)}) copy-start(f32[3,2048,32]{1,2,0:T(8,128)} %reduce-scatter.9.cloned.1.call-done) | copy-start | bytes 2359300
  490.1 58.1 %reduce-scatter.21.cloned.1.call-start = ((), (), s32[]{:S(2)}) async-start(), calls=%async_computation.20 | async-start | bytes 786432 | tf_op jit(solution)/shard_map/reduce_scatter | solution.py:44
  538.3 96.4 %reduce-scatter.23.cloned.1.call-start = ((), (), s32[]{:S(2)}) async-start(), calls=%async_computation.21 | async-start | bytes 4456448 | tf_op jit(solution)/shard_map/reduce_scatter | solution.py:40
  549.9 2.7 copy-start.17
  549.9 2.7 copy-start.18
  549.9 2.7 copy-start.19
  555.3 1.6 copy-start.4
  555.3 145.7 %all-reduce.10.cloned.1.call-start = ((), (), s32[]{:S(2)}) async-start(), calls=%async_computation.22 | async-start | bytes 4587520 | tf_op jit(solution)/shard_map/psum | solution.py:191
  556.9 3.0 copy-start.8
  556.9 3.0 copy-start.23
  561.5 1.6 copy-start.3
  561.5 1.6 copy-start.7
  563.1 1.6 copy-start.1
  567.0 67.7 %copy-start.21 = (f32[512]{0:T(512)S(1)}, f32[512]{0:T(512)}, u32[]{:S(2)}) copy-start(f32[512]{0:T(512)} %param.15) | copy-start | bytes 6148
  567.0 120.8 %copy-start.9 = (f32[128,512]{1,0:T(8,128)S(1)}, f32[128,512]{1,0:T(8,128)}, u32[]{:S(2)}) copy-start(f32[128,512]{1,0:T(8,128)} %get-tuple-element.37) | copy-start | bytes 786436
  701.0 8.3 %copy-start.11 = (f32[512,288]{0,1:T(8,128)S(1)}, f32[512,288]{0,1:T(8,128)}, u32[]{:S(2)}) copy-start(f32[512,288]{0,1:T(8,128)} %get-tuple-element.68) | copy-start | bytes 1769476
  701.0 9.1 %copy-start.10 = (f32[288,512]{1,0:T(8,128)S(1)}, f32[288,512]{1,0:T(8,128)}, u32[]{:S(2)}) copy-start(f32[288,512]{1,0:T(8,128)} %get-tuple-element.69) | copy-start | bytes 1769476
Sparse Core Ops, SparseCore 0:
  12.6 47.7 all-gather.6
  64.3 10.8 reduce-scatter.8
  83.1 79.3 reduce-scatter.10
  164.5 44.4 all-gather.12
  211.6 44.5 all-gather.8
  258.3 11.7 reduce-scatter.16
  272.6 16.7 reduce-scatter.12
  294.2 15.0 all-gather.14
  311.5 13.2 all-gather.10
  328.0 79.1 reduce-scatter.18
  410.9 77.0 reduce-scatter.14
  490.6 44.5 all-gather.16
  538.4 9.6 reduce-scatter.20
  555.4 79.1 reduce-scatter.22
  638.5 62.4 all-reduce.9
where the time goes:
time: 719 us; the launch traced here: 717 us
  waiting for transfers between devices  564 us (78%)
  blocking collectives  63.8 us (9%)
  matrix products  42 us (6%)
  other arithmetic  19.4 us (3%)
  between operations  14.1 us (2%)
  local copies, waits for them, and re-layouts  12.9 us (2%)
    reduce_scatter x4, waiting for transfers between devices, token_total(): return lax.psum_scatter(partial_sum, 'col', scatter_dimension=0, tiled=True)  300 us
    all_gather x4, waiting for transfers between devices, gather_tokens(): return lax.all_gather(values, 'col', axis=0, tiled=True)  178 us
    reduce_scatter x4, waiting for transfers between devices, channel_total(): return lax.psum_scatter(partial_sum, 'row', scatter_dimension=2, tiled=True)  48.6 us
    psum x1, blocking collectives, shards(): lax.psum((first_gain_part, second_gain_part), 'col')  38.2 us
    all_gather x2, waiting for transfers between devices, channel_back(): return lax.all_gather(shares, 'row', axis=2, tiled=True)  24.4 us
  transfers between devices with their start and end apart: 15, of which 15 were waited for; matrix products, arithmetic and copies ran while one was open for 5% of the time, Pallas kernels for 0%

commit v1 on v0

v1 whole, which is shorter than its diff:
```python
import jax
import jax.numpy as jnp
from jax import lax
from jax.experimental import pallas as pl
from jax.experimental.pallas import tpu as pltpu
from jax.sharding import PartitionSpec as P

EPSILON = 1e-05
MESH = pl.DeviceIdType.MESH
F32 = jnp.float32
BF16 = jnp.bfloat16

D = 1024
HALF = 512
CH = 256
CB = 64
FQ = 1152
FB = 288
TC = 256
TO = 64
COPIES = 160


def mod4(value):
    return lax.rem(value + 4, 4)


def nt(a, b):
    return lax.dot_general(a, b, (((1,), (1,)), ((), ())), preferred_element_type=F32)


def nn(a, b):
    return lax.dot_general(a, b, (((1,), (0,)), ((), ())), preferred_element_type=F32)


def tn(a, b):
    return lax.dot_general(a, b, (((0,), (0,)), ((), ())), preferred_element_type=F32)


def loop(count, body):
    def step(i, carry):
        body(i)
        return carry

    lax.fori_loop(0, count, step, 0)


def rows_at(start, size, multiple=32):
    return pl.ds(pl.multiple_of(start, multiple), size)


def lanes_at(start, size):
    return pl.ds(pl.multiple_of(start, 128), size)


def kernel(
    x_in,
    cot_in,
    masks,
    small,
    mix_in,
    gate_in,
    up_in,
    down_in,
    block_o,
    input_o,
    mix_o,
    feed_o,
    stats_o,
    xs,
    cs,
    gains,
    taps_in,
    w_mix,
    w_feed,
    fn,
    pre,
    gat,
    cvd,
    mx,
    res,
    sn,
    gu,
    hid,
    dg,
    fulls,
    halves,
    recvs,
    rg,
    rh,
    cg,
    dm,
    go_f,
    cr_f,
    s_f,
    zr_f,
    xs_f,
    xr_f,
    xf_f,
    go_m,
    cr_m,
    s_m,
    zr_m,
    xs_m,
    xr_m,
    xf_m,
    st,
    st_y,
    st_z,
    st_x,
    bo_own,
    ig_own,
    ss,
    rs,
    ls,
):
    x = lax.axis_index("dp")
    r = lax.axis_index("row")
    col = lax.axis_index("col")
    z = lax.div(col, 4)
    y = lax.rem(col, 4)
    other = 1 - r
    own_lanes = lanes_at(r * HALF, HALF)
    other_lanes = lanes_at(other * HALF, HALF)
    own_rows = rows_at(y * TO, TO)

    def y_peer(d):
        return (x, r, z * 4 + mod4(y + d))

    def z_peer(d):
        return (x, r, mod4(z + d) * 4 + y)

    def x_peer(d):
        return (mod4(x + d), r, col)

    partner = (x, other, col)
    successor = (x, other, mod4(z + r) * 4 + y)
    predecessor = (x, other, mod4(z + r + 3) * 4 + y)
    halo_extra = (x, other, mod4(z + 2 * r - 1) * 4 + y)

    barrier = pltpu.get_barrier_semaphore()
    greeted = [partner, halo_extra]
    for d in (1, 2, 3):
        greeted += [y_peer(d), (x, other, z * 4 + mod4(y + d)), z_peer(d), x_peer(d)]
    for device in greeted:
        pl.semaphore_signal(barrier, inc=1, device_id=device, device_id_type=MESH)
    pl.semaphore_wait(barrier, len(greeted))

    used = [0]
    sent = []

    def slot(count=1):
        first = used[0]
        used[0] += count
        return first

    def push(source, target, device, index=None):
        i = slot() if index is None else index
        copy = pltpu.make_async_remote_copy(
            src_ref=source,
            dst_ref=target,
            send_sem=ss.at[i],
            recv_sem=rs.at[i],
            device_id=device,
            device_id_type=MESH,
        )
        copy.start()
        sent.append((None, copy))
        return copy

    def place(source, target, device, send_index, recv_index, here):
        copy = pltpu.make_async_remote_copy(
            src_ref=source,
            dst_ref=target,
            send_sem=ss.at[send_index],
            recv_sem=rs.at[recv_index],
            device_id=device,
            device_id_type=MESH,
        )

        @pl.when(here)
        def _():
            pltpu.make_async_copy(source, target, rs.at[recv_index]).start()

        @pl.when(jnp.logical_not(here))
        def _():
            copy.start()

        sent.append((here, copy))

    def arrived(source, target, index):
        pltpu.make_async_remote_copy(
            src_ref=source,
            dst_ref=target,
            send_sem=ss.at[index],
            recv_sem=rs.at[index],
            device_id=partner,
            device_id_type=MESH,
        ).wait_recv()

    def tokens_start(source, target):
        base = slot(4)
        core = lax.div(y, 2)
        block = lax.rem(y, 2)
        region = target.at[rows_at(block * 128, 128), own_lanes]
        for d in (1, 3, 2, 0):
            device = (x, core, z * 4 + mod4(y + d))
            index = base + block * 2 + r
            if d:
                copy = pltpu.make_async_remote_copy(
                    src_ref=source,
                    dst_ref=region,
                    send_sem=ss.at[base + d],
                    recv_sem=rs.at[index],
                    device_id=device,
                    device_id_type=MESH,
                )
                copy.start()
                sent.append((None, copy))
            else:
                place(source, region, device, base, index, core == r)
        return base

    def tokens_finish(source, target, base):
        for s in range(4):
            region = target.at[pl.ds((s // 2) * 128, 128), pl.ds((s % 2) * HALF, HALF)]
            arrived(source, region, base + s)

    def owners_start(source, target):
        base = slot(2)
        chip = 2 * r + lax.div(y, 2)
        region = target.at[rows_at(lax.rem(y, 2) * TO, TO)]
        for core in range(2):
            here = jnp.logical_and(chip == y, r == core)
            place(
                source.at[:, pl.ds(core * HALF, HALF)],
                region,
                (x, core, z * 4 + chip),
                base + core,
                base + lax.rem(y, 2),
                here,
            )
        return base

    def owners_finish(source, target, base):
        for s in range(2):
            arrived(source.at[:, pl.ds(0, HALF)], target.at[pl.ds(s * TO, TO)], base + s)

    local = [0]

    class Section:
        def __init__(self, source, region):
            self.source = source
            self.region = region

        def start(self):
            self.z = {d: push(self.source, self.region(z, r), z_peer(d)) for d in (1, 3, 2)}
            self.mine = pltpu.make_async_copy(self.source, self.region(z, r), ls.at[local[0]])
            local[0] += 1
            self.mine.start()
            self.cross = [push(self.source, self.region(z, r), partner)]

        def forward(self):
            for d in (1, 3, 2):
                self.z[d].wait_recv()
                region = self.region(mod4(z - d), r)
                self.cross.append(push(region, region, partner))

        def finish(self):
            self.mine.wait()
            for copy in self.cross:
                copy.wait_recv()

    mix = Section(
        mix_in, lambda zz, rr: w_mix.at[:, rows_at(zz * CB, CB), lanes_at(rr * HALF, HALF)]
    )
    gate = Section(
        gate_in, lambda zz, rr: w_feed.at[rows_at(zz * FB, FB), lanes_at(rr * HALF, HALF)]
    )
    up = Section(
        up_in, lambda zz, rr: w_feed.at[rows_at(FQ + zz * FB, FB), lanes_at(rr * HALF, HALF)]
    )
    down = Section(
        down_in,
        lambda zz, rr: w_feed.at[rows_at(2 * FQ + zz * FB, FB), lanes_at(rr * HALF, HALF)],
    )

    def scatter_start(k):
        return [
            push(halves.at[k, rows_at(mod4(y + d) * TO, TO)], recvs.at[k, d - 1], y_peer(d))
            for d in (1, 3, 2)
        ]

    def scatter_finish(k, copies):
        for copy in copies:
            copy.wait_recv()
        total = fulls[k, own_rows, :]
        for d in range(3):
            total = total + recvs[k, d].astype(F32)
        return total

    def gather_start(buffer):
        return [push(buffer.at[own_rows], buffer.at[own_rows], y_peer(d)) for d in (1, 3, 2)]

    def wait(copies):
        for copy in copies:
            copy.wait_recv()

    def product(k, value):
        def body(n):
            lanes = lanes_at(n * 256, 256)
            part = value(lanes)
            fulls[k, :, lanes] = part
            halves[k, :, lanes] = part.astype(BF16)

        loop(4, body)

    x_base = tokens_start(x_in, xs)
    mix.start()
    small_copies = [push(small, gains.at[:, own_lanes], partner)]
    small_copies += [push(small, taps_in.at[d - 1], z_peer(d)) for d in (1, 3, 2)]
    gains[:, own_lanes] = small[...]
    st[...] = jnp.zeros((8, D), F32)

    tokens_finish(x_in, xs, x_base)
    wait(small_copies)
    cot_base = tokens_start(cot_in, cs)
    first_gain = gains[0:1, :]
    second_gain = gains[1:2, :]
    taps = small[2:5, 0:CH]
    for d in range(3):
        taps = taps + taps_in[d, 2:5, 0:CH]

    def norm_body(i):
        rows = rows_at(i * 32, 32)
        value = xs[rows, :].astype(F32)
        scale = lax.rsqrt(jnp.sum(value * value, axis=1, keepdims=True) / D + EPSILON)
        fn[rows, :] = (value * scale * first_gain).astype(BF16)

    loop(8, norm_body)

    mix.forward()
    gate.start()
    up.start()
    mix.finish()

    def pre_body(s):
        pre[s] = nt(fn[...], w_mix[s])

    loop(3, pre_body)

    gat[8 : 8 + TC, :] = pre[0] * pre[2]
    halo = push(gat.at[pl.ds(TC, 8)], gat.at[pl.ds(0, 8)], successor)
    halo.wait_recv()
    m1 = masks[:, 0:1]
    m2 = masks[:, 1:2]
    cvd[...] = (
        taps[0:1] * gat[8 : 8 + TC, :]
        + taps[1:2] * (m1 * gat[7 : 7 + TC, :])
        + taps[2:3] * (m2 * gat[6 : 6 + TC, :])
    )
    mx[...] = (pre[1] * cvd[...]).astype(BF16)
    product(0, lambda lanes: nn(mx[...], w_mix[3, :, lanes]))
    first_scatter = scatter_start(0)

    residual = xs[own_rows, :].astype(F32) + scatter_finish(0, first_scatter)
    res[...] = residual
    second_scale = lax.rsqrt(jnp.sum(residual * residual, axis=1, keepdims=True) / D + EPSILON)
    sn[own_rows, :] = (residual * second_scale * second_gain).astype(BF16)
    sn_copies = gather_start(sn)

    gate.forward()
    up.forward()
    down.start()
    tokens_finish(cot_in, cs, cot_base)
    gate.finish()
    up.finish()
    wait(sn_copies)

    def gu_body(n):
        at = n * 256
        gu[:, lanes_at(at, 256)] = nt(sn[...], w_feed[rows_at(at, 256), :])

    loop(9, gu_body)

    down.forward()

    def hidden_body(i):
        rows = rows_at(i * 32, 32)
        g = gu[rows, 0:FQ]
        hid[rows, :] = (g * jax.nn.sigmoid(g) * gu[rows, FQ : 2 * FQ]).astype(BF16)

    loop(8, hidden_body)
    down.finish()

    def hg_body(n):
        at = n * 384
        gu[:, lanes_at(2 * FQ + at, 384)] = nt(cs[...], w_feed[rows_at(2 * FQ + at, 384), :])

    loop(3, hg_body)

    def delta_body(i):
        rows = rows_at(i * 32, 32)
        g = gu[rows, 0:FQ]
        u = gu[rows, FQ : 2 * FQ]
        hg = gu[rows, 2 * FQ : 3 * FQ]
        s = jax.nn.sigmoid(g)
        dg[rows, 0:FQ] = (hg * u * s * (1.0 + g * (1.0 - s))).astype(BF16)
        dg[rows, FQ : 2 * FQ] = (hg * (g * s)).astype(BF16)

    loop(8, delta_body)
    product(2, lambda lanes: nn(dg[...], w_feed[0 : 2 * FQ, lanes]))
    grad_scatter = scatter_start(2)
    product(1, lambda lanes: nn(hid[...], w_feed[2 * FQ : 3 * FQ, lanes]))
    block_scatter = scatter_start(1)

    def go_gu_body(n):
        at = n * 384
        go_f[rows_at(at, 384), :] = tn(dg[:, lanes_at(at, 384)], sn[:, other_lanes]).astype(BF16)

    def go_d_body(n):
        at = n * 384
        go_f[rows_at(2 * FQ + at, 384), :] = tn(
            hid[:, lanes_at(at, 384)], cs[:, other_lanes]
        ).astype(BF16)

    loop(6, go_gu_body)
    cross_gu = push(go_f.at[pl.ds(0, 2 * FQ)], cr_f.at[pl.ds(0, 2 * FQ)], partner)
    loop(3, go_d_body)
    cross_d = push(go_f.at[pl.ds(2 * FQ, FQ)], cr_f.at[pl.ds(2 * FQ, FQ)], partner)

    second_grad = scatter_finish(2, grad_scatter)
    residual = res[...]
    second_scale = lax.rsqrt(jnp.sum(residual * residual, axis=1, keepdims=True) / D + EPSILON)
    st[1:2, :] = jnp.sum(second_grad * residual * second_scale, axis=0, keepdims=True)
    weighted = second_grad * second_gain
    cube = second_scale * second_scale * second_scale
    residual_grad = (
        cs[own_rows, :].astype(F32)
        + second_scale * weighted
        - residual * cube * (jnp.sum(weighted * residual, axis=1, keepdims=True) / D)
    )
    rg[...] = residual_grad
    rh[own_rows, :] = residual_grad.astype(BF16)
    rh_copies = gather_start(rh)

    cross_gu.wait_recv()

    def s_gu_body(n):
        at = n * 384
        rows = rows_at(at, 384)
        s_f[rows, :] = (
            tn(dg[:, lanes_at(at, 384)], sn[:, own_lanes]) + cr_f[rows, :].astype(F32)
        ).astype(BF16)

    loop(6, s_gu_body)

    def feed_send(part):
        return [
            push(
                s_f.at[rows_at(part * FQ + mod4(z + d) * FB, FB)],
                zr_f.at[d - 1, pl.ds(part * FB, FB)],
                z_peer(d),
            )
            for d in (1, 3, 2)
        ]

    feed_z = feed_send(0) + feed_send(1)
    cross_d.wait_recv()

    def s_d_body(n):
        at = n * 384
        rows = rows_at(2 * FQ + at, 384)
        s_f[rows, :] = (
            tn(hid[:, lanes_at(at, 384)], cs[:, own_lanes]) + cr_f[rows, :].astype(F32)
        ).astype(BF16)

    loop(3, s_d_body)
    feed_z += feed_send(2)

    wait(rh_copies)
    mixed_grad = nt(rh[...], w_mix[3])
    cg[0:TC, :] = mixed_grad * pre[1]
    halo_back = push(cg.at[pl.ds(0, 8)], cg.at[pl.ds(TC, 8)], predecessor)
    dm[1] = (mixed_grad * cvd[...]).astype(BF16)

    def grad_rows(s, first, lanes):
        return tn(first, lanes)

    go_m[3] = tn(mx[...], rh[:, other_lanes]).astype(BF16)

    conv_grad = cg[0:TC, :]
    tap_lanes = lanes_at(y * CH, CH)
    st[2:3, tap_lanes] = jnp.sum(conv_grad * gat[8 : 8 + TC, :], axis=0, keepdims=True)
    st[3:4, tap_lanes] = jnp.sum(conv_grad * m1 * gat[7 : 7 + TC, :], axis=0, keepdims=True)
    st[4:5, tap_lanes] = jnp.sum(conv_grad * m2 * gat[6 : 6 + TC, :], axis=0, keepdims=True)
    halo_back.wait_recv()
    gated_grad = (
        taps[0:1] * conv_grad
        + taps[1:2] * (masks[:, 2:3] * cg[1 : 1 + TC, :])
        + taps[2:3] * (masks[:, 3:4] * cg[2 : 2 + TC, :])
    )
    dm[0] = (gated_grad * pre[2]).astype(BF16)
    dm[2] = (gated_grad * pre[0]).astype(BF16)

    def first_part(lanes):
        part = nn(dm[0], w_mix[0, :, lanes])
        part = part + nn(dm[1], w_mix[1, :, lanes])
        return part + nn(dm[2], w_mix[2, :, lanes])

    product(3, first_part)
    first_scatter = scatter_start(3)

    def go_m_body(s):
        go_m[s] = tn(dm[s], fn[:, other_lanes]).astype(BF16)

    loop(3, go_m_body)
    cross_m = push(go_m, cr_m, partner)

    bo_own[...] = (res[...] + scatter_finish(1, block_scatter)).astype(BF16)
    bo_base = owners_start(bo_own, block_o)

    cross_m.wait_recv()

    def s_m_body(s):
        s_m[s] = (tn(dm[s], fn[:, own_lanes]) + cr_m[s].astype(F32)).astype(BF16)

    loop(3, s_m_body)
    s_m[3] = (tn(mx[...], rh[:, own_lanes]) + cr_m[3].astype(F32)).astype(BF16)
    mix_z = [
        push(s_m.at[:, rows_at(mod4(z + d) * CB, CB), :], zr_m.at[d - 1], z_peer(d))
        for d in (1, 3, 2)
    ]

    wait(feed_z)
    for part in range(3):
        mine = s_f[rows_at(part * FQ + z * FB, FB), :].astype(F32)
        at = part * FB
        for d in range(3):
            mine = mine + zr_f[d, at : at + FB, :].astype(F32)
        xs_f[at : at + FB, :] = mine.astype(BF16)
    feed_x = [
        push(xs_f.at[:, lanes_at(mod4(x + d) * 128, 128)], xr_f.at[d - 1], x_peer(d))
        for d in (1, 3, 2)
    ]

    first_grad = scatter_finish(3, first_scatter)
    value = xs[own_rows, :].astype(F32)
    first_scale = lax.rsqrt(jnp.sum(value * value, axis=1, keepdims=True) / D + EPSILON)
    st[0:1, :] = jnp.sum(first_grad * value * first_scale, axis=0, keepdims=True)
    weighted = first_grad * first_gain
    cube = first_scale * first_scale * first_scale
    ig_own[...] = (
        rg[...]
        + first_scale * weighted
        - value * cube * (jnp.sum(weighted * value, axis=1, keepdims=True) / D)
    )
    ig_base = owners_start(ig_own, input_o)
    stat_copies = [push(st, st_y.at[0], partner)]
    for d in (1, 2, 3):
        stat_copies.append(push(st, st_y.at[2 * d - 1], y_peer(d)))
        stat_copies.append(push(st, st_y.at[2 * d], (x, other, z * 4 + mod4(y + d))))

    x_lanes = lanes_at(x * 128, 128)
    wait(feed_x)
    mine = xs_f[:, x_lanes].astype(F32)
    for d in range(3):
        mine = mine + xr_f[d].astype(F32)
    xf_f[:, x_lanes] = mine.astype(BF16)
    feed_g = [push(xf_f.at[:, x_lanes], xf_f.at[:, x_lanes], x_peer(d)) for d in (1, 3, 2)]

    wait(stat_copies)
    total = st[...]
    for i in range(7):
        total = total + st_y[i]
    st_z[3] = total
    stat_copies = [push(st_z.at[3], st_z.at[d - 1], z_peer(d)) for d in (1, 3, 2)]

    wait(mix_z)
    mine = s_m[:, rows_at(z * CB, CB), :].astype(F32)
    for d in range(3):
        mine = mine + zr_m[d].astype(F32)
    xs_m[...] = mine.astype(BF16)
    mix_x = [
        push(xs_m.at[:, :, lanes_at(mod4(x + d) * 128, 128)], xr_m.at[d - 1], x_peer(d))
        for d in (1, 3, 2)
    ]
    wait(stat_copies)
    st_x[3] = st_z[0] + st_z[1] + st_z[2] + st_z[3]
    stat_copies = [push(st_x.at[3], st_x.at[d - 1], x_peer(d)) for d in (1, 3, 2)]

    wait(mix_x)
    mine = xs_m[:, :, x_lanes].astype(F32)
    for d in range(3):
        mine = mine + xr_m[d].astype(F32)
    xf_m[:, :, x_lanes] = mine.astype(BF16)
    mix_g = [push(xf_m.at[:, :, x_lanes], xf_m.at[:, :, x_lanes], x_peer(d)) for d in (1, 3, 2)]

    wait(feed_g)
    feed_o[...] = xf_f[...].astype(F32)
    owners_finish(bo_own, block_o, bo_base)
    owners_finish(ig_own, input_o, ig_base)
    wait(stat_copies)
    stats_o[...] = st_x[0] + st_x[1] + st_x[2] + st_x[3]
    wait(mix_g)
    mix_o[...] = xf_m[...].astype(F32)

    for here, copy in sent:
        if here is None:
            copy.wait_send()
        else:

            @pl.when(jnp.logical_not(here))
            def _(copy=copy):
                copy.wait_send()


def shards(
    hidden_in,
    segment_ids,
    first_gain,
    mixer_b,
    mixer_c,
    mixer_v,
    conv_kernel,
    mixer_out,
    second_gain,
    gate_weight,
    up_weight,
    down_weight,
    cotangent,
):
    r = lax.axis_index("row")
    col = lax.axis_index("col")
    z = col // 4
    y = col % 4
    ids = segment_ids[0]
    length = ids.shape[0]
    outside = jnp.full((2,), -1, jnp.int32)
    padded = jnp.concatenate([outside, ids, outside - 1])
    m1 = padded[1 : 1 + length] == ids
    m2 = padded[:length] == ids
    n1 = padded[3 : 3 + length] == ids
    n2 = padded[4 : 4 + length] == ids
    masks = jnp.stack([m1, m2, n1, n2], 1).astype(F32)
    masks = lax.dynamic_slice_in_dim(masks, z * 512 + r * TC, TC, 0)
    masks = jnp.pad(masks, ((0, 0), (0, 124)))
    tap_rows = lax.dynamic_update_slice(jnp.zeros((3, HALF), F32), conv_kernel, (0, z * CB))
    small = jnp.concatenate(
        [first_gain[None], second_gain[None], tap_rows, jnp.zeros((3, HALF), F32)], 0
    )
    mix = jnp.stack([mixer_b.T, mixer_c.T, mixer_v.T, mixer_out], 0)
    vmem = pl.BlockSpec(memory_space=pltpu.VMEM)
    shape = jax.ShapeDtypeStruct
    scratch = [
        ((TC, D), BF16),
        ((TC, D), BF16),
        ((8, D), F32),
        ((3, 8, HALF), F32),
        ((4, CH, D), BF16),
        ((3 * FQ, D), BF16),
        ((TC, D), BF16),
        ((3, TC, CH), F32),
        ((TC + 8, CH), F32),
        ((TC, CH), F32),
        ((TC, CH), BF16),
        ((TO, D), F32),
        ((TC, D), BF16),
        ((TC, 3 * FQ), F32),
        ((TC, FQ), BF16),
        ((TC, 2 * FQ), BF16),
        ((4, TC, D), F32),
        ((4, TC, D), BF16),
        ((4, 3, TO, D), BF16),
        ((TO, D), F32),
        ((TC, D), BF16),
        ((TC + 8, CH), F32),
        ((3, TC, CH), BF16),
        ((3 * FQ, HALF), BF16),
        ((3 * FQ, HALF), BF16),
        ((3 * FQ, HALF), BF16),
        ((3, 3 * FB, HALF), BF16),
        ((3 * FB, HALF), BF16),
        ((3, 3 * FB, 128), BF16),
        ((3 * FB, HALF), BF16),
        ((4, CH, HALF), BF16),
        ((4, CH, HALF), BF16),
        ((4, CH, HALF), BF16),
        ((3, 4, CB, HALF), BF16),
        ((4, CB, HALF), BF16),
        ((3, 4, CB, 128), BF16),
        ((4, CB, HALF), BF16),
        ((8, D), F32),
        ((7, 8, D), F32),
        ((4, 8, D), F32),
        ((4, 8, D), F32),
        ((TO, D), BF16),
        ((TO, D), F32),
    ]
    block_out, input_grad, mix_grad, feed_grad, stats = pl.pallas_call(
        kernel,
        out_shape=(
            shape((128, HALF), BF16),
            shape((128, HALF), F32),
            shape((4, CB, HALF), F32),
            shape((3 * FB, HALF), F32),
            shape((8, D), F32),
        ),
        in_specs=[vmem] * 8,
        out_specs=(vmem,) * 5,
        scratch_shapes=[pltpu.VMEM(s, t) for s, t in scratch]
        + [
            pltpu.SemaphoreType.DMA((COPIES,)),
            pltpu.SemaphoreType.DMA((COPIES,)),
            pltpu.SemaphoreType.DMA((4,)),
        ],
        compiler_params=pltpu.CompilerParams(
            collective_id=0, has_side_effects=True, vmem_limit_bytes=62 * 2**20
        ),
    )(
        hidden_in,
        cotangent,
        masks,
        small,
        mix,
        gate_weight.T,
        up_weight.T,
        down_weight,
    )
    mine = lax.dynamic_slice_in_dim(stats[:2], r * HALF, HALF, 1)
    kernel_grad = lax.dynamic_slice(stats, (2, y * CH + z * CB + r * 32), (3, 32))
    return (
        block_out,
        input_grad,
        mine[0],
        mix_grad[0].T,
        mix_grad[1].T,
        mix_grad[2].T,
        kernel_grad,
        mix_grad[3],
        mine[1],
        feed_grad[:FB].T,
        feed_grad[FB : 2 * FB].T,
        feed_grad[2 * FB :],
    )


def solution(mesh):
    return jax.shard_map(
        shards,
        mesh=mesh,
        in_specs=(
            P(("dp", "col"), "row"),
            P("dp", None),
            P("row"),
            P("row", "col"),
            P("row", "col"),
            P("row", "col"),
            P(None, "col"),
            P("col", "row"),
            P("row"),
            P("row", "col"),
            P("row", "col"),
            P("col", "row"),
            P(("dp", "col"), "row"),
        ),
        out_specs=(
            P(("dp", "col"), "row"),
            P(("dp", "col"), "row"),
            P("row"),
            P("row", "col"),
            P("row", "col"),
            P("row", "col"),
            P(None, ("col", "row")),
            P("col", "row"),
            P("row"),
            P("row", "col"),
            P("row", "col"),
            P("col", "row"),
        ),
        check_vma=False,
    )
```

time: 719 us -> 176 us (0.24)
  waiting for transfers between devices: 564 us -> 0 us
  Pallas kernels: 0 us -> 161 us
  blocking collectives: 63.8 us -> 0 us
  matrix products: 42 us -> 0 us
  other arithmetic: 19.4 us -> 4.03 us
  between operations: 14.1 us -> 0.75 us
    reduce_scatter x8 -> x0, waiting for transfers between devices: 349 us -> none  [the longest x4 300 us: token_total(): return lax.psum_scatter(partial_sum, 'col', scatter_dimension=0, tiled=True)]
    all_gather x6 -> x0, waiting for transfers between devices: 203 us -> none  [the longest x4 178 us: gather_tokens(): return lax.all_gather(values, 'col', axis=0, tiled=True)]
    pallas_call x0 -> x1, Pallas kernels: none -> 161 us  [shards(): pl.pallas_call(kernel, out_shape=(shape((128, HALF), BF16), shape((128, H...]
    psum x6 -> x0, blocking collectives: 59.4 us -> none  [the longest x1 38.2 us: shards(): lax.psum((first_gain_part, second_gain_part), 'col')]
    dot_general x15 -> x0, matrix products: 42 us -> none  [the longest x1 5.45 us: shards(): jnp.einsum('ktf,kdf->td', feed_delta, feed_stack, preferred_element_type=...]
    psum x1 -> x0, waiting for transfers between devices: 11.5 us -> none  [shards(): lax.psum((first_gain_grad, mixer_b_grad, mixer_c_grad, mixer_v_grad, kern...]
    unnamed x55 -> x7, local copies, waits for them, and re-layouts: 12.5 us -> 1.5 us
    convert_element_type x8 -> x1, other arithmetic: 9.62 us -> 0.09 us  [shards(): masks = jnp.stack([m1, m2, n1, n2], 1).astype(F32)]
  transfers between devices with their start and end apart: 15 -> 0, of which waited for: 15 -> 0; matrix products, arithmetic and copies ran while one was open for 5% -> 0% of each run, Pallas kernels for 0% -> 0%
where the time goes in v1:
time: 176 us
  Pallas kernels  161 us (91%)
  local copies, waits for them, and re-layouts  10.4 us (6%)
  other arithmetic  4.03 us (2%)
    pallas_call x1, Pallas kernels, shards(): pl.pallas_call(kernel, out_shape=(shape((128, HALF), BF16), shape((128, H...  161 us

profile of v1, /device:TPU:0, one launch (start us, length us, event | category | flops | bytes accessed | tf_op | source)
XLA Modules:
  0.0 175.8 jit_solution(303820587688428214)
XLA Ops:
  0.7 0.8 dynamic_update_slice.3
  1.5 1.3 pad_maximum_fusion.1.small
  2.8 1.0 fusion
  3.9 0.1 fusion.7
  4.0 0.1 copy.30
  4.1 0.7 pad.8.masks
  4.8 1.7 pad_maximum_fusion.mix_in
  6.4 160.7 %shard_map.220 = (bf16[128,512]{1,0:T(8,128)(2,1)}, f32[128,512]{1,0:T(8,128)}, f32[4,64,512]{2,1,0:T(8,128)}, f32[864,512]{1,0:T(8,128)}, f32[8,1024]{1,0:T(8,128)}) custom-call(bf16[128,512]{1,0:T(8,128)(2,1)} %x_in.1, bf16[128,512]{1,0:T(8,128)(2,1)} %cot_in.1, f32[256,128]{1,0:T(8,128)} %pad.8.masks, f32[8,512]{1,0:T(8,128)} %pad_maximum_fusion.1.small, ...), custom_call_target="tpu_custom_call" | custom-call | tf_op jit(solution)/shard_map/pallas_call | solution.py:700
  167.1 1.3 constant_dynamic-slice_fusion.1
  168.4 0.8 slice.50
  169.2 0.7 fusion.9
  169.8 1.9 %slice_bitcast_fusion.2 = (f32[64,512]{1,0:T(8,128)}, f32[512,64]{0,1:T(8,128)}, f32[512,64]{0,1:T(8,128)}, f32[512,64]{0,1:T(8,128)}) fusion(f32[4,64,512]{2,1,0:T(8,128)} %get-tuple-element.20), kind=kLoop, calls=%fused_computation.3 | loop fusion | bytes 1048576 | tf_op jit(solution)/shard_map/squeeze | solution.py:740
  171.7 0.0 copy-start.1
  171.7 0.0 copy-start
  171.7 2.7 %fusion.8 = (f32[288,512]{1,0:T(8,128)}, f32[512,288]{0,1:T(8,128)}, f32[512,288]{0,1:T(8,128)}) fusion(f32[864,512]{1,0:T(8,128)} %get-tuple-element.21), kind=kLoop, calls=%fused_computation.26 | loop fusion | bytes 3538944 | tf_op jit(solution)/shard_map/slice | solution.py:744
  174.4 0.0 copy-done.1
  174.5 0.7 copy.35
  175.1 0.0 copy-done
  175.1 0.7 copy.36
  (6 shorter events, 0.1 us)
Async XLA Ops:
  171.7 2.7 %copy-start.1 = (bf16[128,512]{1,0:T(8,128)(2,1)S(1)}, bf16[128,512]{1,0:T(8,128)(2,1)}, u32[]{:S(2)}) copy-start(bf16[128,512]{1,0:T(8,128)(2,1)} %get-tuple-element.47) | copy-start | bytes 393220
  171.7 3.4 %copy-start = (f32[128,512]{1,0:T(8,128)S(1)}, f32[128,512]{1,0:T(8,128)}, u32[]{:S(2)}) copy-start(f32[128,512]{1,0:T(8,128)} %get-tuple-element.48) | copy-start | bytes 786436

commit v2 on v1

--- a/solution.py
+++ b/solution.py
@@ -18,7 +18,7 @@
 FB = 288
 TC = 256
 TO = 64
-COPIES = 160
+COPIES = 256
 
 
 def mod4(value):
@@ -56,17 +56,29 @@
 def kernel(
     x_in,
     cot_in,
-    masks,
-    small,
-    mix_in,
+    ids,
+    first_in,
+    second_in,
+    taps_own,
+    b_in,
+    c_in,
+    v_in,
+    out_in,
     gate_in,
     up_in,
     down_in,
     block_o,
     input_o,
-    mix_o,
-    feed_o,
+    b_o,
+    c_o,
+    v_o,
+    out_o,
+    gate_o,
+    up_o,
+    down_o,
     stats_o,
+    small,
+    masks,
     xs,
     cs,
     gains,
@@ -97,6 +109,9 @@
     xs_f,
     xr_f,
     xf_f,
+    x1_d,
+    t_d,
+    z2_d,
     go_m,
     cr_m,
     s_m,
@@ -104,6 +119,9 @@
     xs_m,
     xr_m,
     xf_m,
+    x1_m,
+    t_m,
+    z2_m,
     st,
     st_y,
     st_z,
@@ -271,18 +289,57 @@
             for copy in self.cross:
                 copy.wait_recv()
 
-    mix = Section(
-        mix_in, lambda zz, rr: w_mix.at[:, rows_at(zz * CB, CB), lanes_at(rr * HALF, HALF)]
-    )
+    class Split:
+        def __init__(self, source, region):
+            self.source = source
+            self.region = region
+
+        def start(self):
+            quarter = self.source.at[:, lanes_at(x * 128, 128)]
+            self.z = {
+                d: push(quarter, self.region(z, r * HALF + x * 128, 128), z_peer(d))
+                for d in (1, 3, 2)
+            }
+            whole = self.region(z, r * HALF, HALF)
+            self.mine = pltpu.make_async_copy(self.source, whole, ls.at[local[0]])
+            local[0] += 1
+            self.mine.start()
+            self.cross = [push(self.source, whole, partner)]
+
+        def forward(self):
+            self.x = []
+            for d in (1, 3, 2):
+                self.z[d].wait_recv()
+                region = self.region(mod4(z - d), r * HALF + x * 128, 128)
+                self.x += [push(region, region, x_peer(e)) for e in (1, 3, 2)]
+
+        def across(self):
+            for copy in self.x:
+                copy.wait_recv()
+            for d in (1, 3, 2):
+                region = self.region(mod4(z - d), r * HALF, HALF)
+                self.cross.append(push(region, region, partner))
+
+        def finish(self):
+            self.mine.wait()
+            for copy in self.cross:
+                copy.wait_recv()
+
+    def mix_section(s, source):
+        return Section(
+            source, lambda zz, rr: w_mix.at[s, rows_at(zz * CB, CB), lanes_at(rr * HALF, HALF)]
+        )
+
+    mix = [mix_section(s, source) for s, source in enumerate((b_in, c_in, v_in, out_in))]
     gate = Section(
         gate_in, lambda zz, rr: w_feed.at[rows_at(zz * FB, FB), lanes_at(rr * HALF, HALF)]
     )
-    up = Section(
-        up_in, lambda zz, rr: w_feed.at[rows_at(FQ + zz * FB, FB), lanes_at(rr * HALF, HALF)]
-    )
-    down = Section(
+    up = Split(
+        up_in, lambda zz, at, size: w_feed.at[rows_at(FQ + zz * FB, FB), lanes_at(at, size)]
+    )
+    down = Split(
         down_in,
-        lambda zz, rr: w_feed.at[rows_at(2 * FQ + zz * FB, FB), lanes_at(rr * HALF, HALF)],
+        lambda zz, at, size: w_feed.at[rows_at(2 * FQ + zz * FB, FB), lanes_at(at, size)],
     )
 
     def scatter_start(k):
@@ -315,12 +372,20 @@
 
         loop(4, body)
 
+    small[0:1, :] = first_in[...]
+    small[1:2, :] = second_in[...]
+    small[2:5, 0:CH] = taps_own[...]
     x_base = tokens_start(x_in, xs)
-    mix.start()
+    for section in mix:
+        section.start()
+    up.start()
     small_copies = [push(small, gains.at[:, own_lanes], partner)]
     small_copies += [push(small, taps_in.at[d - 1], z_peer(d)) for d in (1, 3, 2)]
     gains[:, own_lanes] = small[...]
     st[...] = jnp.zeros((8, D), F32)
+    here = ids[2 : 2 + TC, :]
+    for k, first in enumerate((1, 0, 3, 4)):
+        masks[k] = (ids[first : first + TC, :] == here).astype(F32)
 
     tokens_finish(x_in, xs, x_base)
     wait(small_copies)
@@ -339,10 +404,13 @@
 
     loop(8, norm_body)
 
-    mix.forward()
+    for section in mix:
+        section.forward()
+    down.start()
     gate.start()
-    up.start()
-    mix.finish()
+    up.forward()
+    for section in mix:
+        section.finish()
 
     def pre_body(s):
         pre[s] = nt(fn[...], w_mix[s])
@@ -352,8 +420,8 @@
     gat[8 : 8 + TC, :] = pre[0] * pre[2]
     halo = push(gat.at[pl.ds(TC, 8)], gat.at[pl.ds(0, 8)], successor)
     halo.wait_recv()
-    m1 = masks[:, 0:1]
-    m2 = masks[:, 1:2]
+    m1 = masks[0, :, 0:1]
+    m2 = masks[1, :, 0:1]
     cvd[...] = (
         taps[0:1] * gat[8 : 8 + TC, :]
         + taps[1:2] * (m1 * gat[7 : 7 + TC, :])
@@ -362,6 +430,7 @@
     mx[...] = (pre[1] * cvd[...]).astype(BF16)
     product(0, lambda lanes: nn(mx[...], w_mix[3, :, lanes]))
     first_scatter = scatter_start(0)
+    down.forward()
 
     residual = xs[own_rows, :].astype(F32) + scatter_finish(0, first_scatter)
     res[...] = residual
@@ -370,8 +439,7 @@
     sn_copies = gather_start(sn)
 
     gate.forward()
-    up.forward()
-    down.start()
+    up.across()
     tokens_finish(cot_in, cs, cot_base)
     gate.finish()
     up.finish()
@@ -383,7 +451,7 @@
 
     loop(9, gu_body)
 
-    down.forward()
+    down.across()
 
     def hidden_body(i):
         rows = rows_at(i * 32, 32)
@@ -429,6 +497,28 @@
     loop(3, go_d_body)
     cross_d = push(go_f.at[pl.ds(2 * FQ, FQ)], cr_f.at[pl.ds(2 * FQ, FQ)], partner)
 
+    cross_gu.wait_recv()
+
+    def s_gu_body(n):
+        at = n * 384
+        rows = rows_at(at, 384)
+        s_f[rows, :] = (
+            tn(dg[:, lanes_at(at, 384)], sn[:, own_lanes]) + cr_f[rows, :].astype(F32)
+        ).astype(BF16)
+
+    loop(6, s_gu_body)
+
+    def feed_send(part):
+        return [
+            push(
+                s_f.at[rows_at(part * FQ + mod4(z + d) * FB, FB)],
+                zr_f.at[d - 1, pl.ds(part * FB, FB)],
+                z_peer(d),
+            )
+            for d in (1, 3, 2)
+        ]
+
+    feed_z = feed_send(0) + feed_send(1)
     second_grad = scatter_finish(2, grad_scatter)
     residual = res[...]
     second_scale = lax.rsqrt(jnp.sum(residual * residual, axis=1, keepdims=True) / D + EPSILON)
@@ -444,28 +534,6 @@
     rh[own_rows, :] = residual_grad.astype(BF16)
     rh_copies = gather_start(rh)
 
-    cross_gu.wait_recv()
-
-    def s_gu_body(n):
-        at = n * 384
-        rows = rows_at(at, 384)
-        s_f[rows, :] = (
-            tn(dg[:, lanes_at(at, 384)], sn[:, own_lanes]) + cr_f[rows, :].astype(F32)
-        ).astype(BF16)
-
-    loop(6, s_gu_body)
-
-    def feed_send(part):
-        return [
-            push(
-                s_f.at[rows_at(part * FQ + mod4(z + d) * FB, FB)],
-                zr_f.at[d - 1, pl.ds(part * FB, FB)],
-                z_peer(d),
-            )
-            for d in (1, 3, 2)
-        ]
-
-    feed_z = feed_send(0) + feed_send(1)
     cross_d.wait_recv()
 
     def s_d_body(n):
@@ -476,16 +544,16 @@
         ).astype(BF16)
 
     loop(3, s_d_body)
-    feed_z += feed_send(2)
+    down_x = [
+        push(s_f.at[pl.ds(2 * FQ, FQ), lanes_at(mod4(x + d) * 128, 128)], x1_d.at[d - 1], x_peer(d))
+        for d in (1, 3, 2)
+    ]
 
     wait(rh_copies)
     mixed_grad = nt(rh[...], w_mix[3])
     cg[0:TC, :] = mixed_grad * pre[1]
     halo_back = push(cg.at[pl.ds(0, 8)], cg.at[pl.ds(TC, 8)], predecessor)
     dm[1] = (mixed_grad * cvd[...]).astype(BF16)
-
-    def grad_rows(s, first, lanes):
-        return tn(first, lanes)
 
     go_m[3] = tn(mx[...], rh[:, other_lanes]).astype(BF16)
 
@@ -497,8 +565,8 @@
     halo_back.wait_recv()
     gated_grad = (
         taps[0:1] * conv_grad
-        + taps[1:2] * (masks[:, 2:3] * cg[1 : 1 + TC, :])
-        + taps[2:3] * (masks[:, 3:4] * cg[2 : 2 + TC, :])
+        + taps[1:2] * (masks[2, :, 0:1] * cg[1 : 1 + TC, :])
+        + taps[2:3] * (masks[3, :, 0:1] * cg[2 : 2 + TC, :])
     )
     dm[0] = (gated_grad * pre[2]).astype(BF16)
     dm[2] = (gated_grad * pre[0]).astype(BF16)
@@ -517,8 +585,15 @@
     loop(3, go_m_body)
     cross_m = push(go_m, cr_m, partner)
 
-    bo_own[...] = (res[...] + scatter_finish(1, block_scatter)).astype(BF16)
-    bo_base = owners_start(bo_own, block_o)
+    x_lanes = lanes_at(x * 128, 128)
+    wait(down_x)
+    mine = s_f[2 * FQ : 3 * FQ, x_lanes].astype(F32)
+    for d in range(3):
+        mine = mine + x1_d[d].astype(F32)
+    t_d[...] = mine.astype(BF16)
+    down_z = [
+        push(t_d.at[rows_at(mod4(z + d) * FB, FB)], z2_d.at[d - 1], z_peer(d)) for d in (1, 3, 2)
+    ]
 
     cross_m.wait_recv()
 
@@ -528,12 +603,16 @@
     loop(3, s_m_body)
     s_m[3] = (tn(mx[...], rh[:, own_lanes]) + cr_m[3].astype(F32)).astype(BF16)
     mix_z = [
-        push(s_m.at[:, rows_at(mod4(z + d) * CB, CB), :], zr_m.at[d - 1], z_peer(d))
+        push(s_m.at[0:2, rows_at(mod4(z + d) * CB, CB), :], zr_m.at[d - 1], z_peer(d))
         for d in (1, 3, 2)
     ]
+    mix_x = [
+        push(s_m.at[2:4, :, lanes_at(mod4(x + d) * 128, 128)], x1_m.at[d - 1], x_peer(d))
+        for d in (1, 3, 2)
+    ]
 
     wait(feed_z)
-    for part in range(3):
+    for part in range(2):
         mine = s_f[rows_at(part * FQ + z * FB, FB), :].astype(F32)
         at = part * FB
         for d in range(3):
@@ -543,6 +622,9 @@
         push(xs_f.at[:, lanes_at(mod4(x + d) * 128, 128)], xr_f.at[d - 1], x_peer(d))
         for d in (1, 3, 2)
     ]
+
+    bo_own[...] = (res[...] + scatter_finish(1, block_scatter)).astype(BF16)
+    bo_base = owners_start(bo_own, block_o)
 
     first_grad = scatter_finish(3, first_scatter)
     value = xs[own_rows, :].astype(F32)
@@ -561,12 +643,35 @@
         stat_copies.append(push(st, st_y.at[2 * d - 1], y_peer(d)))
         stat_copies.append(push(st, st_y.at[2 * d], (x, other, z * 4 + mod4(y + d))))
 
-    x_lanes = lanes_at(x * 128, 128)
+    wait(mix_x)
+    mine = s_m[2:4, :, x_lanes].astype(F32)
+    for d in range(3):
+        mine = mine + x1_m[d].astype(F32)
+    t_m[...] = mine.astype(BF16)
+    mix_zz = [
+        push(t_m.at[:, rows_at(mod4(z + d) * CB, CB), :], z2_m.at[d - 1], z_peer(d))
+        for d in (1, 3, 2)
+    ]
+    wait(mix_z)
+    mine = s_m[0:2, rows_at(z * CB, CB), :].astype(F32)
+    for d in range(3):
+        mine = mine + zr_m[d].astype(F32)
+    xs_m[...] = mine.astype(BF16)
+    mix_xx = [
+        push(xs_m.at[:, :, lanes_at(mod4(x + d) * 128, 128)], xr_m.at[d - 1], x_peer(d))
+        for d in (1, 3, 2)
+    ]
+
     wait(feed_x)
     mine = xs_f[:, x_lanes].astype(F32)
     for d in range(3):
         mine = mine + xr_f[d].astype(F32)
-    xf_f[:, x_lanes] = mine.astype(BF16)
+    xf_f[0 : 2 * FB, x_lanes] = mine.astype(BF16)
+    wait(down_z)
+    mine = t_d[rows_at(z * FB, FB), :].astype(F32)
+    for d in range(3):
+        mine = mine + z2_d[d].astype(F32)
+    xf_f[2 * FB : 3 * FB, x_lanes] = mine.astype(BF16)
     feed_g = [push(xf_f.at[:, x_lanes], xf_f.at[:, x_lanes], x_peer(d)) for d in (1, 3, 2)]
 
     wait(stat_copies)
@@ -576,34 +681,32 @@
     st_z[3] = total
     stat_copies = [push(st_z.at[3], st_z.at[d - 1], z_peer(d)) for d in (1, 3, 2)]
 
-    wait(mix_z)
-    mine = s_m[:, rows_at(z * CB, CB), :].astype(F32)
+    wait(mix_zz)
+    mine = t_m[:, rows_at(z * CB, CB), :].astype(F32)
     for d in range(3):
-        mine = mine + zr_m[d].astype(F32)
-    xs_m[...] = mine.astype(BF16)
-    mix_x = [
-        push(xs_m.at[:, :, lanes_at(mod4(x + d) * 128, 128)], xr_m.at[d - 1], x_peer(d))
-        for d in (1, 3, 2)
-    ]
+        mine = mine + z2_m[d].astype(F32)
+    xf_m[2:4, :, x_lanes] = mine.astype(BF16)
+    wait(mix_xx)
+    mine = xs_m[:, :, x_lanes].astype(F32)
+    for d in range(3):
+        mine = mine + xr_m[d].astype(F32)
+    xf_m[0:2, :, x_lanes] = mine.astype(BF16)
+    mix_g = [push(xf_m.at[:, :, x_lanes], xf_m.at[:, :, x_lanes], x_peer(d)) for d in (1, 3, 2)]
+
     wait(stat_copies)
     st_x[3] = st_z[0] + st_z[1] + st_z[2] + st_z[3]
     stat_copies = [push(st_x.at[3], st_x.at[d - 1], x_peer(d)) for d in (1, 3, 2)]
 
-    wait(mix_x)
-    mine = xs_m[:, :, x_lanes].astype(F32)
-    for d in range(3):
-        mine = mine + xr_m[d].astype(F32)
-    xf_m[:, :, x_lanes] = mine.astype(BF16)
-    mix_g = [push(xf_m.at[:, :, x_lanes], xf_m.at[:, :, x_lanes], x_peer(d)) for d in (1, 3, 2)]
-
-    wait(feed_g)
-    feed_o[...] = xf_f[...].astype(F32)
     owners_finish(bo_own, block_o, bo_base)
     owners_finish(ig_own, input_o, ig_base)
+    wait(feed_g)
+    for part, target in enumerate((gate_o, up_o, down_o)):
+        target[...] = xf_f[part * FB : (part + 1) * FB, :].astype(F32)
+    wait(mix_g)
+    for part, target in enumerate((b_o, c_o, v_o, out_o)):
+        target[...] = xf_m[part].astype(F32)
     wait(stat_copies)
     stats_o[...] = st_x[0] + st_x[1] + st_x[2] + st_x[3]
-    wait(mix_g)
-    mix_o[...] = xf_m[...].astype(F32)
 
     for here, copy in sent:
         if here is None:
@@ -634,25 +737,16 @@
     col = lax.axis_index("col")
     z = col // 4
     y = col % 4
-    ids = segment_ids[0]
-    length = ids.shape[0]
-    outside = jnp.full((2,), -1, jnp.int32)
-    padded = jnp.concatenate([outside, ids, outside - 1])
-    m1 = padded[1 : 1 + length] == ids
-    m2 = padded[:length] == ids
-    n1 = padded[3 : 3 + length] == ids
-    n2 = padded[4 : 4 + length] == ids
-    masks = jnp.stack([m1, m2, n1, n2], 1).astype(F32)
-    masks = lax.dynamic_slice_in_dim(masks, z * 512 + r * TC, TC, 0)
-    masks = jnp.pad(masks, ((0, 0), (0, 124)))
-    tap_rows = lax.dynamic_update_slice(jnp.zeros((3, HALF), F32), conv_kernel, (0, z * CB))
-    small = jnp.concatenate(
-        [first_gain[None], second_gain[None], tap_rows, jnp.zeros((3, HALF), F32)], 0
-    )
-    mix = jnp.stack([mixer_b.T, mixer_c.T, mixer_v.T, mixer_out], 0)
+    ids = jnp.pad(segment_ids[0], ((2, 6),), constant_values=-1)
+    ids = lax.dynamic_slice_in_dim(ids, z * 512 + r * TC, TC + 8, 0)
+    ids = jnp.broadcast_to(ids[:, None], (TC + 8, 128))
+    at_z = lax.broadcasted_iota(jnp.int32, (3, CH), 1) // CB == z
+    taps = jnp.where(at_z, jnp.tile(conv_kernel, (1, CH // CB)), 0.0)
     vmem = pl.BlockSpec(memory_space=pltpu.VMEM)
     shape = jax.ShapeDtypeStruct
     scratch = [
+        ((8, HALF), F32),
+        ((4, TC, 128), F32),
         ((TC, D), BF16),
         ((TC, D), BF16),
         ((8, D), F32),
@@ -679,17 +773,23 @@
         ((3 * FQ, HALF), BF16),
         ((3 * FQ, HALF), BF16),
         ((3 * FQ, HALF), BF16),
-        ((3, 3 * FB, HALF), BF16),
+        ((3, 2 * FB, HALF), BF16),
+        ((2 * FB, HALF), BF16),
+        ((3, 2 * FB, 128), BF16),
         ((3 * FB, HALF), BF16),
-        ((3, 3 * FB, 128), BF16),
-        ((3 * FB, HALF), BF16),
+        ((3, FQ, 128), BF16),
+        ((FQ, 128), BF16),
+        ((3, FB, 128), BF16),
         ((4, CH, HALF), BF16),
         ((4, CH, HALF), BF16),
         ((4, CH, HALF), BF16),
-        ((3, 4, CB, HALF), BF16),
+        ((3, 2, CB, HALF), BF16),
+        ((2, CB, HALF), BF16),
+        ((3, 2, CB, 128), BF16),
         ((4, CB, HALF), BF16),
-        ((3, 4, CB, 128), BF16),
-        ((4, CB, HALF), BF16),
+        ((3, 2, CH, 128), BF16),
+        ((2, CH, 128), BF16),
+        ((3, 2, CB, 128), BF16),
         ((8, D), F32),
         ((7, 8, D), F32),
         ((4, 8, D), F32),
@@ -697,22 +797,22 @@
         ((TO, D), BF16),
         ((TO, D), F32),
     ]
-    block_out, input_grad, mix_grad, feed_grad, stats = pl.pallas_call(
+    block_out, input_grad, b_g, c_g, v_g, out_g, gate_g, up_g, down_g, stats = pl.pallas_call(
         kernel,
         out_shape=(
             shape((128, HALF), BF16),
             shape((128, HALF), F32),
-            shape((4, CB, HALF), F32),
-            shape((3 * FB, HALF), F32),
+            *[shape((CB, HALF), F32)] * 4,
+            *[shape((FB, HALF), F32)] * 3,
             shape((8, D), F32),
         ),
-        in_specs=[vmem] * 8,
-        out_specs=(vmem,) * 5,
+        in_specs=[vmem] * 13,
+        out_specs=(vmem,) * 10,
         scratch_shapes=[pltpu.VMEM(s, t) for s, t in scratch]
         + [
             pltpu.SemaphoreType.DMA((COPIES,)),
             pltpu.SemaphoreType.DMA((COPIES,)),
-            pltpu.SemaphoreType.DMA((4,)),
+            pltpu.SemaphoreType.DMA((7,)),
         ],
         compiler_params=pltpu.CompilerParams(
             collective_id=0, has_side_effects=True, vmem_limit_bytes=62 * 2**20
@@ -720,9 +820,14 @@
     )(
         hidden_in,
         cotangent,
-        masks,
-        small,
-        mix,
+        ids,
+        first_gain[None],
+        second_gain[None],
+        taps,
+        mixer_b.T,
+        mixer_c.T,
+        mixer_v.T,
+        mixer_out,
         gate_weight.T,
         up_weight.T,
         down_weight,
@@ -733,15 +838,15 @@
         block_out,
         input_grad,
         mine[0],
-        mix_grad[0].T,
-        mix_grad[1].T,
-        mix_grad[2].T,
+        b_g.T,
+        c_g.T,
+        v_g.T,
         kernel_grad,
-        mix_grad[3],
+        out_g,
         mine[1],
-        feed_grad[:FB].T,
-        feed_grad[FB : 2 * FB].T,
-        feed_grad[2 * FB :],
+        gate_g.T,
+        up_g.T,
+        down_g,
     )
 
 

time: 176 us -> 158 us (0.90)
  Pallas kernels: 161 us -> 143 us
  local copies, waits for them, and re-layouts: 10.4 us -> 13.9 us
  other arithmetic: 4.03 us -> 0.61 us
    pallas_call x1, Pallas kernels: 161 us -> 143 us  [shards(): pl.pallas_call(kernel, out_shape=(shape((128, HALF), BF16), shape((128, H...]
    unnamed x7 -> x29, local copies, waits for them, and re-layouts: 1.5 us -> 10.2 us
    slice x1 -> x0, local copies, waits for them, and re-layouts: 2.71 us -> none  [shards(): feed_grad[2 * FB:]]
    squeeze x1 -> x0, local copies, waits for them, and re-layouts: 1.89 us -> none  [shards(): mix_grad[3]]
where the time goes in v2:
time: 158 us
  Pallas kernels  143 us (91%)
  local copies, waits for them, and re-layouts  13.9 us (9%)
    pallas_call x1, Pallas kernels, shards(): pl.pallas_call(kernel, out_shape=(shape((128, HALF), BF16), shape((128, H...  143 us
    unnamed x29, local copies, waits for them, and re-layouts  10.2 us

profile of v2, /device:TPU:0, one launch (start us, length us, event | category | flops | bytes accessed | tf_op | source)
XLA Modules:
  0.0 157.8 jit_solution(12009673013926401458)
XLA Ops:
  0.7 0.0 copy-start.8
  0.7 0.7 copy-done.8
  1.4 0.1 pad_dynamic-slice_fusion
  1.5 0.0 copy-start.9
  1.5 0.7 copy-done.9
  2.1 0.1 tile.10
  2.2 0.6 fusion.taps_own
  2.8 0.8 broadcast_in_dim.16.ids
  3.6 142.5 %shard_map.220 = (bf16[128,512]{1,0:T(8,128)(2,1)}, f32[128,512]{1,0:T(8,128)}, f32[64,512]{1,0:T(8,128)}, f32[64,512]{1,0:T(8,128)}, f32[64,512]{1,0:T(8,128)},...) custom-call(bf16[128,512]{1,0:T(8,128)(2,1)} %x_in.1, ...), custom_call_target="tpu_custom_call" | custom-call | tf_op jit(solution)/shard_map/pallas_call | solution.py:800
  146.1 0.0 copy-start.3
  146.1 1.4 constant_dynamic-slice_fusion
  147.5 0.8 slice.9
  148.3 0.7 fusion.1
  148.9 1.6 copy.34
  150.5 0.0 copy-done.3
  150.5 0.0 copy-start.7
  150.5 0.0 copy-start.6
  150.5 0.0 copy-start.5
  150.5 0.7 copy.35
  151.2 0.3 copy-done.7
  151.5 0.0 copy-start.2
  151.5 0.7 copy.36
  152.2 0.0 copy-done.6
  152.2 0.7 copy.37
  152.8 0.0 copy-done.5
  152.8 0.0 copy-start.4
  152.8 0.7 copy.38
  153.5 0.3 copy-done.4
  153.8 0.7 copy.39
  154.4 0.0 copy-done.2
  154.4 0.0 copy-start.1
  154.4 0.8 copy.40
  155.2 0.5 copy-done.1
  155.7 0.0 copy-start
  155.7 0.8 copy.41
  156.5 0.5 copy-done
  157.0 0.8 copy.42
  (3 shorter events, 0.0 us)
Async XLA Ops:
  0.7 0.7 copy-start.8
  1.5 0.7 copy-start.9
  146.1 4.4 %copy-start.3 = (f32[128,512]{1,0:T(8,128)S(1)}, f32[128,512]{1,0:T(8,128)}, u32[]{:S(2)}) copy-start(f32[128,512]{1,0:T(8,128)} %get-tuple-element.49) | copy-start | bytes 786436
  150.5 1.0 copy-start.7
  150.5 1.7 %copy-start.6 = (f32[64,512]{1,0:T(8,128)S(1)}, f32[64,512]{1,0:T(8,128)}, u32[]{:S(2)}) copy-start(f32[64,512]{1,0:T(8,128)} %get-tuple-element.26) | copy-start | bytes 393220
  150.5 2.3 %copy-start.5 = (f32[64,512]{1,0:T(8,128)S(1)}, f32[64,512]{1,0:T(8,128)}, u32[]{:S(2)}) copy-start(f32[64,512]{1,0:T(8,128)} %get-tuple-element.27) | copy-start | bytes 393220
  151.5 2.9 %copy-start.2 = (f32[288,512]{1,0:T(8,128)S(1)}, f32[288,512]{1,0:T(8,128)}, u32[]{:S(2)}) copy-start(f32[288,512]{1,0:T(8,128)} %get-tuple-element.29) | copy-start | bytes 1769476
  152.8 1.0 copy-start.4
  154.4 1.3 copy-start.1
  155.7 1.3 copy-start

commit v3 on v2

--- a/solution.py
+++ b/solution.py
@@ -69,13 +69,8 @@
     down_in,
     block_o,
     input_o,
-    b_o,
-    c_o,
-    v_o,
-    out_o,
-    gate_o,
-    up_o,
-    down_o,
+    mix_o,
+    feed_o,
     stats_o,
     small,
     masks,
@@ -119,9 +114,6 @@
     xs_m,
     xr_m,
     xf_m,
-    x1_m,
-    t_m,
-    z2_m,
     st,
     st_y,
     st_z,
@@ -479,9 +471,6 @@
     loop(8, delta_body)
     product(2, lambda lanes: nn(dg[...], w_feed[0 : 2 * FQ, lanes]))
     grad_scatter = scatter_start(2)
-    product(1, lambda lanes: nn(hid[...], w_feed[2 * FQ : 3 * FQ, lanes]))
-    block_scatter = scatter_start(1)
-
     def go_gu_body(n):
         at = n * 384
         go_f[rows_at(at, 384), :] = tn(dg[:, lanes_at(at, 384)], sn[:, other_lanes]).astype(BF16)
@@ -548,6 +537,8 @@
         push(s_f.at[pl.ds(2 * FQ, FQ), lanes_at(mod4(x + d) * 128, 128)], x1_d.at[d - 1], x_peer(d))
         for d in (1, 3, 2)
     ]
+    product(1, lambda lanes: nn(hid[...], w_feed[2 * FQ : 3 * FQ, lanes]))
+    block_scatter = scatter_start(1)
 
     wait(rh_copies)
     mixed_grad = nt(rh[...], w_mix[3])
@@ -595,22 +586,6 @@
         push(t_d.at[rows_at(mod4(z + d) * FB, FB)], z2_d.at[d - 1], z_peer(d)) for d in (1, 3, 2)
     ]
 
-    cross_m.wait_recv()
-
-    def s_m_body(s):
-        s_m[s] = (tn(dm[s], fn[:, own_lanes]) + cr_m[s].astype(F32)).astype(BF16)
-
-    loop(3, s_m_body)
-    s_m[3] = (tn(mx[...], rh[:, own_lanes]) + cr_m[3].astype(F32)).astype(BF16)
-    mix_z = [
-        push(s_m.at[0:2, rows_at(mod4(z + d) * CB, CB), :], zr_m.at[d - 1], z_peer(d))
-        for d in (1, 3, 2)
-    ]
-    mix_x = [
-        push(s_m.at[2:4, :, lanes_at(mod4(x + d) * 128, 128)], x1_m.at[d - 1], x_peer(d))
-        for d in (1, 3, 2)
-    ]
-
     wait(feed_z)
     for part in range(2):
         mine = s_f[rows_at(part * FQ + z * FB, FB), :].astype(F32)
@@ -622,6 +597,35 @@
         push(xs_f.at[:, lanes_at(mod4(x + d) * 128, 128)], xr_f.at[d - 1], x_peer(d))
         for d in (1, 3, 2)
     ]
+
+    cross_m.wait_recv()
+
+    def s_m_body(s):
+        s_m[s] = (tn(dm[s], fn[:, own_lanes]) + cr_m[s].astype(F32)).astype(BF16)
+
+    loop(3, s_m_body)
+    s_m[3] = (tn(mx[...], rh[:, own_lanes]) + cr_m[3].astype(F32)).astype(BF16)
+    mix_z = [
+        push(s_m.at[:, rows_at(mod4(z + d) * CB, CB), :], zr_m.at[d - 1], z_peer(d))
+        for d in (1, 3, 2)
+    ]
+
+    kept = []
+
+    def spread(source, target):
+        copy = pltpu.make_async_copy(source, target, ls.at[local[0]])
+        local[0] += 1
+        copy.start()
+        kept.append(copy)
+        return [push(source, target, x_peer(d)) for d in (1, 3, 2)]
+
+    wait(down_z)
+    mine = t_d[rows_at(z * FB, FB), :].astype(F32)
+    for d in range(3):
+        mine = mine + z2_d[d].astype(F32)
+    xf_f[2 * FB : 3 * FB, :] = mine.astype(BF16)
+    down_rows = pl.ds(2 * FB, FB)
+    feed_g = spread(xf_f.at[down_rows], feed_o.at[down_rows, x_lanes])
 
     bo_own[...] = (res[...] + scatter_finish(1, block_scatter)).astype(BF16)
     bo_base = owners_start(bo_own, block_o)
@@ -643,36 +647,13 @@
         stat_copies.append(push(st, st_y.at[2 * d - 1], y_peer(d)))
         stat_copies.append(push(st, st_y.at[2 * d], (x, other, z * 4 + mod4(y + d))))
 
-    wait(mix_x)
-    mine = s_m[2:4, :, x_lanes].astype(F32)
-    for d in range(3):
-        mine = mine + x1_m[d].astype(F32)
-    t_m[...] = mine.astype(BF16)
-    mix_zz = [
-        push(t_m.at[:, rows_at(mod4(z + d) * CB, CB), :], z2_m.at[d - 1], z_peer(d))
-        for d in (1, 3, 2)
-    ]
-    wait(mix_z)
-    mine = s_m[0:2, rows_at(z * CB, CB), :].astype(F32)
-    for d in range(3):
-        mine = mine + zr_m[d].astype(F32)
-    xs_m[...] = mine.astype(BF16)
-    mix_xx = [
-        push(xs_m.at[:, :, lanes_at(mod4(x + d) * 128, 128)], xr_m.at[d - 1], x_peer(d))
-        for d in (1, 3, 2)
-    ]
-
     wait(feed_x)
     mine = xs_f[:, x_lanes].astype(F32)
     for d in range(3):
         mine = mine + xr_f[d].astype(F32)
-    xf_f[0 : 2 * FB, x_lanes] = mine.astype(BF16)
-    wait(down_z)
-    mine = t_d[rows_at(z * FB, FB), :].astype(F32)
-    for d in range(3):
-        mine = mine + z2_d[d].astype(F32)
-    xf_f[2 * FB : 3 * FB, x_lanes] = mine.astype(BF16)
-    feed_g = [push(xf_f.at[:, x_lanes], xf_f.at[:, x_lanes], x_peer(d)) for d in (1, 3, 2)]
+    xf_f[0 : 2 * FB, :] = mine.astype(BF16)
+    gate_rows = pl.ds(0, 2 * FB)
+    feed_g += spread(xf_f.at[gate_rows], feed_o.at[gate_rows, x_lanes])
 
     wait(stat_copies)
     total = st[...]
@@ -681,32 +662,34 @@
     st_z[3] = total
     stat_copies = [push(st_z.at[3], st_z.at[d - 1], z_peer(d)) for d in (1, 3, 2)]
 
-    wait(mix_zz)
-    mine = t_m[:, rows_at(z * CB, CB), :].astype(F32)
+    wait(mix_z)
+    mine = s_m[:, rows_at(z * CB, CB), :].astype(F32)
     for d in range(3):
-        mine = mine + z2_m[d].astype(F32)
-    xf_m[2:4, :, x_lanes] = mine.astype(BF16)
-    wait(mix_xx)
+        mine = mine + zr_m[d].astype(F32)
+    xs_m[...] = mine.astype(BF16)
+    mix_x = [
+        push(xs_m.at[:, :, lanes_at(mod4(x + d) * 128, 128)], xr_m.at[d - 1], x_peer(d))
+        for d in (1, 3, 2)
+    ]
+    wait(stat_copies)
+    st_x[3] = st_z[0] + st_z[1] + st_z[2] + st_z[3]
+    stat_copies = [push(st_x.at[3], st_x.at[d - 1], x_peer(d)) for d in (1, 3, 2)]
+
+    wait(mix_x)
     mine = xs_m[:, :, x_lanes].astype(F32)
     for d in range(3):
         mine = mine + xr_m[d].astype(F32)
-    xf_m[0:2, :, x_lanes] = mine.astype(BF16)
-    mix_g = [push(xf_m.at[:, :, x_lanes], xf_m.at[:, :, x_lanes], x_peer(d)) for d in (1, 3, 2)]
+    xf_m[...] = mine.astype(BF16)
+    mix_g = spread(xf_m, mix_o.at[:, :, x_lanes])
 
     wait(stat_copies)
-    st_x[3] = st_z[0] + st_z[1] + st_z[2] + st_z[3]
-    stat_copies = [push(st_x.at[3], st_x.at[d - 1], x_peer(d)) for d in (1, 3, 2)]
-
+    stats_o[...] = st_x[0] + st_x[1] + st_x[2] + st_x[3]
     owners_finish(bo_own, block_o, bo_base)
     owners_finish(ig_own, input_o, ig_base)
     wait(feed_g)
-    for part, target in enumerate((gate_o, up_o, down_o)):
-        target[...] = xf_f[part * FB : (part + 1) * FB, :].astype(F32)
     wait(mix_g)
-    for part, target in enumerate((b_o, c_o, v_o, out_o)):
-        target[...] = xf_m[part].astype(F32)
-    wait(stat_copies)
-    stats_o[...] = st_x[0] + st_x[1] + st_x[2] + st_x[3]
+    for copy in kept:
+        copy.wait()
 
     for here, copy in sent:
         if here is None:
@@ -716,6 +699,46 @@
             @pl.when(jnp.logical_not(here))
             def _(copy=copy):
                 copy.wait_send()
+
+
+def finish(
+    block_i,
+    input_i,
+    mix_i,
+    feed_i,
+    stats,
+    block_o,
+    input_o,
+    b_o,
+    c_o,
+    v_o,
+    out_o,
+    gate_o,
+    up_o,
+    down_o,
+    first_o,
+    second_o,
+    taps_o,
+):
+    r = lax.axis_index("row")
+    col = lax.axis_index("col")
+    z = lax.div(col, 4)
+    y = lax.rem(col, 4)
+    block_o[...] = block_i[...]
+    input_o[...] = input_i[...]
+    lanes = lanes_at(r * HALF, HALF)
+    first_o[...] = stats[0:1, lanes]
+    second_o[...] = stats[1:2, lanes]
+    window = stats[2:5, lanes_at(y * CH + lax.div(z, 2) * 128, 128)]
+    place = lax.rem(z, 2) * 2 + r
+    total = jnp.zeros((3, 32), F32)
+    for k in range(4):
+        total = total + jnp.where(place == k, window[:, k * 32 : (k + 1) * 32], 0.0)
+    taps_o[...] = total
+    for part, target in enumerate((gate_o, up_o, down_o)):
+        target[...] = feed_i[part * FB : (part + 1) * FB, :].astype(F32)
+    for part, target in enumerate((b_o, c_o, v_o, out_o)):
+        target[...] = mix_i[part].astype(F32)
 
 
 def shards(
@@ -743,6 +766,7 @@
     at_z = lax.broadcasted_iota(jnp.int32, (3, CH), 1) // CB == z
     taps = jnp.where(at_z, jnp.tile(conv_kernel, (1, CH // CB)), 0.0)
     vmem = pl.BlockSpec(memory_space=pltpu.VMEM)
+    whole = pl.BlockSpec(memory_space=pl.ANY)
     shape = jax.ShapeDtypeStruct
     scratch = [
         ((8, HALF), F32),
@@ -776,20 +800,17 @@
         ((3, 2 * FB, HALF), BF16),
         ((2 * FB, HALF), BF16),
         ((3, 2 * FB, 128), BF16),
-        ((3 * FB, HALF), BF16),
+        ((3 * FB, 128), BF16),
         ((3, FQ, 128), BF16),
         ((FQ, 128), BF16),
         ((3, FB, 128), BF16),
         ((4, CH, HALF), BF16),
         ((4, CH, HALF), BF16),
         ((4, CH, HALF), BF16),
-        ((3, 2, CB, HALF), BF16),
-        ((2, CB, HALF), BF16),
-        ((3, 2, CB, 128), BF16),
+        ((3, 4, CB, HALF), BF16),
         ((4, CB, HALF), BF16),
-        ((3, 2, CH, 128), BF16),
-        ((2, CH, 128), BF16),
-        ((3, 2, CB, 128), BF16),
+        ((3, 4, CB, 128), BF16),
+        ((4, CB, 128), BF16),
         ((8, D), F32),
         ((7, 8, D), F32),
         ((4, 8, D), F32),
@@ -797,22 +818,22 @@
         ((TO, D), BF16),
         ((TO, D), F32),
     ]
-    block_out, input_grad, b_g, c_g, v_g, out_g, gate_g, up_g, down_g, stats = pl.pallas_call(
+    results = pl.pallas_call(
         kernel,
         out_shape=(
             shape((128, HALF), BF16),
             shape((128, HALF), F32),
-            *[shape((CB, HALF), F32)] * 4,
-            *[shape((FB, HALF), F32)] * 3,
+            shape((4, CB, HALF), BF16),
+            shape((3 * FB, HALF), BF16),
             shape((8, D), F32),
         ),
-        in_specs=[vmem] * 13,
-        out_specs=(vmem,) * 10,
+        in_specs=[whole] * 2 + [vmem] * 4 + [whole] * 7,
+        out_specs=(whole,) * 4 + (vmem,),
         scratch_shapes=[pltpu.VMEM(s, t) for s, t in scratch]
         + [
             pltpu.SemaphoreType.DMA((COPIES,)),
             pltpu.SemaphoreType.DMA((COPIES,)),
-            pltpu.SemaphoreType.DMA((7,)),
+            pltpu.SemaphoreType.DMA((10,)),
         ],
         compiler_params=pltpu.CompilerParams(
             collective_id=0, has_side_effects=True, vmem_limit_bytes=62 * 2**20
@@ -832,18 +853,26 @@
         up_weight.T,
         down_weight,
     )
-    mine = lax.dynamic_slice_in_dim(stats[:2], r * HALF, HALF, 1)
-    kernel_grad = lax.dynamic_slice(stats, (2, y * CH + z * CB + r * 32), (3, 32))
+    copied = [((128, HALF), BF16), ((128, HALF), F32)]
+    small_out = [((1, HALF), F32), ((1, HALF), F32), ((3, 32), F32)]
+    grads = [((CB, HALF), F32)] * 4 + [((FB, HALF), F32)] * 3
+    outs = pl.pallas_call(
+        finish,
+        out_shape=tuple(shape(a, t) for a, t in copied + grads + small_out),
+        in_specs=[vmem] * 5,
+        out_specs=(vmem,) * 12,
+    )(*results)
+    block_out, input_grad, b_g, c_g, v_g, out_g, gate_g, up_g, down_g, first_g, second_g, taps_g = outs
     return (
         block_out,
         input_grad,
-        mine[0],
+        first_g[0],
         b_g.T,
         c_g.T,
         v_g.T,
-        kernel_grad,
+        taps_g,
         out_g,
-        mine[1],
+        second_g[0],
         gate_g.T,
         up_g.T,
         down_g,

time: 158 us -> 142 us (0.90); the launches traced: 158 us -> 139 us
  local copies, waits for them, and re-layouts: 13.9 us -> 2.28 us
  Pallas kernels: 143 us -> 136 us
    pallas_call x1, Pallas kernels: 143 us -> 133 us  [shards(): pl.pallas_call(kernel, out_shape=(shape((128, HALF), BF16), shape((128, H...]
    unnamed x29 -> x4, local copies, waits for them, and re-layouts: 10.2 us -> 1.36 us
    pallas_call x0 -> x1, Pallas kernels: none -> 2.89 us  [shards(): pl.pallas_call(finish, out_shape=tuple((shape(a, t) for a, t in copied +...]
where the time goes in v3:
time: 142 us; the launch traced here: 139 us
  Pallas kernels  136 us (96%)
  local copies, waits for them, and re-layouts  2.28 us (2%)
    pallas_call x1, Pallas kernels, shards(): pl.pallas_call(kernel, out_shape=(shape((128, HALF), BF16), shape((128, H...  133 us
    pallas_call x1, Pallas kernels, shards(): pl.pallas_call(finish, out_shape=tuple((shape(a, t) for a, t in copied +...  2.89 us

profile of v3, /device:TPU:0, one launch (start us, length us, event | category | flops | bytes accessed | tf_op | source)
XLA Modules:
  0.0 139.3 jit_solution(11266140179153269134)
XLA Ops:
  0.7 0.0 copy-start
  0.7 0.7 copy-done
  1.4 0.1 pad_dynamic-slice_fusion
  1.4 0.0 copy-start.1
  1.4 0.7 copy-done.1
  2.1 0.1 tile.10
  2.2 0.6 fusion.taps_own
  2.8 0.8 broadcast_in_dim.16.ids
  3.6 132.8 %shard_map.220 = (bf16[128,512]{1,0:T(8,128)(2,1)}, f32[128,512]{1,0:T(8,128)}, bf16[4,64,512]{2,1,0:T(8,128)(2,1)}, bf16[864,512]{1,0:T(8,128)(2,1)}, f32[8,1024]{1,0:T(8,128)}) custom-call(bf16[128,512]{1,0:T(8,128)(2,1)} %x_in.1, bf16[128,512]{1,0:T(8,128)(2,1)} %cot_in.1, s32[264,128]{1,0:T(8,128)} %broadcast_in_dim.16.ids, f32[1,512]{1,0:T(1,128)} %bitcast.21, ...), custom_call_target="tpu_custom_call" | custom-call | tf_op jit(solution)/shard_map/pallas_call | solution.py:821
  136.4 2.9 %shard_map.221 = (bf16[128,512]{1,0:T(8,128)(2,1)}, f32[128,512]{1,0:T(8,128)}, f32[64,512]{1,0:T(8,128)}, f32[64,512]{1,0:T(8,128)}, f32[64,512]{1,0:T(8,128)},...) custom-call(bf16[128,512]{1,0:T(8,128)(2,1)} %get-tuple-element.29.b, ...), custom_call_target="tpu_custom_call" | custom-call | tf_op jit(solution)/shard_map/pallas_call | solution.py:859
  (3 shorter events, 0.0 us)
Async XLA Ops:
  0.7 0.7 copy-start
  1.4 0.7 copy-start.1

commit v4 on v3

--- a/solution.py
+++ b/solution.py
@@ -398,8 +398,6 @@
 
     for section in mix:
         section.forward()
-    down.start()
-    gate.start()
     up.forward()
     for section in mix:
         section.finish()
@@ -412,6 +410,8 @@
     gat[8 : 8 + TC, :] = pre[0] * pre[2]
     halo = push(gat.at[pl.ds(TC, 8)], gat.at[pl.ds(0, 8)], successor)
     halo.wait_recv()
+    down.start()
+    gate.start()
     m1 = masks[0, :, 0:1]
     m2 = masks[1, :, 0:1]
     cvd[...] = (

time: 142 us -> 134 us (0.944); the launches traced: 139 us -> 133 us
  Pallas kernels: 136 us -> 130 us
    pallas_call x1, Pallas kernels: 133 us -> 127 us  [shards(): pl.pallas_call(kernel, out_shape=(shape((128, HALF), BF16), shape((128, H...]
where the time goes in v4:
time: 134 us; the launch traced here: 133 us
  Pallas kernels  130 us (97%)
  local copies, waits for them, and re-layouts  2.28 us (2%)
    pallas_call x1, Pallas kernels, shards(): pl.pallas_call(kernel, out_shape=(shape((128, HALF), BF16), shape((128, H...  127 us
    pallas_call x1, Pallas kernels, shards(): pl.pallas_call(finish, out_shape=tuple((shape(a, t) for a, t in copied +...  2.89 us

profile of v4, /device:TPU:0, one launch (start us, length us, event | category | flops | bytes accessed | tf_op | source)
XLA Modules:
  0.0 133.3 jit_solution(8383428912239485409)
XLA Ops:
  0.7 0.0 copy-start
  0.7 0.7 copy-done
  1.4 0.1 pad_dynamic-slice_fusion
  1.4 0.0 copy-start.1
  1.4 0.7 copy-done.1
  2.1 0.1 tile.10
  2.2 0.6 fusion.taps_own
  2.8 0.8 broadcast_in_dim.16.ids
  3.6 126.9 %shard_map.220 = (bf16[128,512]{1,0:T(8,128)(2,1)}, f32[128,512]{1,0:T(8,128)}, bf16[4,64,512]{2,1,0:T(8,128)(2,1)}, bf16[864,512]{1,0:T(8,128)(2,1)}, f32[8,1024]{1,0:T(8,128)}) custom-call(bf16[128,512]{1,0:T(8,128)(2,1)} %x_in.1, bf16[128,512]{1,0:T(8,128)(2,1)} %cot_in.1, s32[264,128]{1,0:T(8,128)} %broadcast_in_dim.16.ids, f32[1,512]{1,0:T(1,128)} %bitcast.21, ...), custom_call_target="tpu_custom_call" | custom-call | tf_op jit(solution)/shard_map/pallas_call | solution.py:821
  130.5 2.9 %shard_map.221 = (bf16[128,512]{1,0:T(8,128)(2,1)}, f32[128,512]{1,0:T(8,128)}, f32[64,512]{1,0:T(8,128)}, f32[64,512]{1,0:T(8,128)}, f32[64,512]{1,0:T(8,128)},...) custom-call(bf16[128,512]{1,0:T(8,128)(2,1)} %get-tuple-element.29.b, ...), custom_call_target="tpu_custom_call" | custom-call | tf_op jit(solution)/shard_map/pallas_call | solution.py:859
  (3 shorter events, 0.0 us)
Async XLA Ops:
  0.7 0.7 copy-start
  1.4 0.7 copy-start.1

commit v5 on v4

--- a/solution.py
+++ b/solution.py
@@ -507,7 +507,7 @@
             for d in (1, 3, 2)
         ]
 
-    feed_z = feed_send(0) + feed_send(1)
+    feed_z = feed_send(0)
     second_grad = scatter_finish(2, grad_scatter)
     residual = res[...]
     second_scale = lax.rsqrt(jnp.sum(residual * residual, axis=1, keepdims=True) / D + EPSILON)
@@ -554,6 +554,7 @@
     st[3:4, tap_lanes] = jnp.sum(conv_grad * m1 * gat[7 : 7 + TC, :], axis=0, keepdims=True)
     st[4:5, tap_lanes] = jnp.sum(conv_grad * m2 * gat[6 : 6 + TC, :], axis=0, keepdims=True)
     halo_back.wait_recv()
+    feed_z += feed_send(1)
     gated_grad = (
         taps[0:1] * conv_grad
         + taps[1:2] * (masks[2, :, 0:1] * cg[1 : 1 + TC, :])
@@ -586,6 +587,18 @@
         push(t_d.at[rows_at(mod4(z + d) * FB, FB)], z2_d.at[d - 1], z_peer(d)) for d in (1, 3, 2)
     ]
 
+    cross_m.wait_recv()
+
+    def s_m_body(s):
+        s_m[s] = (tn(dm[s], fn[:, own_lanes]) + cr_m[s].astype(F32)).astype(BF16)
+
+    loop(3, s_m_body)
+    s_m[3] = (tn(mx[...], rh[:, own_lanes]) + cr_m[3].astype(F32)).astype(BF16)
+    mix_z = [
+        push(s_m.at[:, rows_at(mod4(z + d) * CB, CB), :], zr_m.at[d - 1], z_peer(d))
+        for d in (1, 3, 2)
+    ]
+
     wait(feed_z)
     for part in range(2):
         mine = s_f[rows_at(part * FQ + z * FB, FB), :].astype(F32)
@@ -595,18 +608,6 @@
         xs_f[at : at + FB, :] = mine.astype(BF16)
     feed_x = [
         push(xs_f.at[:, lanes_at(mod4(x + d) * 128, 128)], xr_f.at[d - 1], x_peer(d))
-        for d in (1, 3, 2)
-    ]
-
-    cross_m.wait_recv()
-
-    def s_m_body(s):
-        s_m[s] = (tn(dm[s], fn[:, own_lanes]) + cr_m[s].astype(F32)).astype(BF16)
-
-    loop(3, s_m_body)
-    s_m[3] = (tn(mx[...], rh[:, own_lanes]) + cr_m[3].astype(F32)).astype(BF16)
-    mix_z = [
-        push(s_m.at[:, rows_at(mod4(z + d) * CB, CB), :], zr_m.at[d - 1], z_peer(d))
         for d in (1, 3, 2)
     ]
 

time: 134 us -> 133 us (level)
  Pallas kernels: 130 us -> 128 us
    pallas_call x1, Pallas kernels: 127 us -> 125 us  [shards(): pl.pallas_call(kernel, out_shape=(shape((128, HALF), BF16), shape((128, H...]
where the time goes in v5:
time: 133 us; the launch traced here: 131 us
  Pallas kernels  128 us (96%)
  local copies, waits for them, and re-layouts  2.28 us (2%)
    pallas_call x1, Pallas kernels, shards(): pl.pallas_call(kernel, out_shape=(shape((128, HALF), BF16), shape((128, H...  125 us
    pallas_call x1, Pallas kernels, shards(): pl.pallas_call(finish, out_shape=tuple((shape(a, t) for a, t in copied +...  2.89 us

profile of v5, /device:TPU:0, one launch (start us, length us, event | category | flops | bytes accessed | tf_op | source)
XLA Modules:
  0.0 131.1 jit_solution(4025682815871792698)
XLA Ops:
  0.7 0.0 copy-start
  0.7 0.7 copy-done
  1.4 0.1 pad_dynamic-slice_fusion
  1.4 0.0 copy-start.1
  1.4 0.7 copy-done.1
  2.1 0.1 tile.10
  2.2 0.6 fusion.taps_own
  2.8 0.8 broadcast_in_dim.16.ids
  3.6 124.6 %shard_map.220 = (bf16[128,512]{1,0:T(8,128)(2,1)}, f32[128,512]{1,0:T(8,128)}, bf16[4,64,512]{2,1,0:T(8,128)(2,1)}, bf16[864,512]{1,0:T(8,128)(2,1)}, f32[8,1024]{1,0:T(8,128)}) custom-call(bf16[128,512]{1,0:T(8,128)(2,1)} %x_in.1, bf16[128,512]{1,0:T(8,128)(2,1)} %cot_in.1, s32[264,128]{1,0:T(8,128)} %broadcast_in_dim.16.ids, f32[1,512]{1,0:T(1,128)} %bitcast.21, ...), custom_call_target="tpu_custom_call" | custom-call | tf_op jit(solution)/shard_map/pallas_call | solution.py:822
  128.2 2.9 %shard_map.221 = (bf16[128,512]{1,0:T(8,128)(2,1)}, f32[128,512]{1,0:T(8,128)}, f32[64,512]{1,0:T(8,128)}, f32[64,512]{1,0:T(8,128)}, f32[64,512]{1,0:T(8,128)},...) custom-call(bf16[128,512]{1,0:T(8,128)(2,1)} %get-tuple-element.29.b, ...), custom_call_target="tpu_custom_call" | custom-call | tf_op jit(solution)/shard_map/pallas_call | solution.py:860
  (3 shorter events, 0.0 us)
Async XLA Ops:
  0.7 0.7 copy-start
  1.4 0.7 copy-start.1

commit v6 on v5

--- a/solution.py
+++ b/solution.py
@@ -370,7 +370,6 @@
     x_base = tokens_start(x_in, xs)
     for section in mix:
         section.start()
-    up.start()
     small_copies = [push(small, gains.at[:, own_lanes], partner)]
     small_copies += [push(small, taps_in.at[d - 1], z_peer(d)) for d in (1, 3, 2)]
     gains[:, own_lanes] = small[...]
@@ -398,7 +397,6 @@
 
     for section in mix:
         section.forward()
-    up.forward()
     for section in mix:
         section.finish()
 
@@ -410,6 +408,7 @@
     gat[8 : 8 + TC, :] = pre[0] * pre[2]
     halo = push(gat.at[pl.ds(TC, 8)], gat.at[pl.ds(0, 8)], successor)
     halo.wait_recv()
+    up.start()
     down.start()
     gate.start()
     m1 = masks[0, :, 0:1]
@@ -422,6 +421,7 @@
     mx[...] = (pre[1] * cvd[...]).astype(BF16)
     product(0, lambda lanes: nn(mx[...], w_mix[3, :, lanes]))
     first_scatter = scatter_start(0)
+    up.forward()
     down.forward()
 
     residual = xs[own_rows, :].astype(F32) + scatter_finish(0, first_scatter)

time: 133 us -> 134 us (level)
  no operation moved by 1% of the time
where the time goes in v6:
time: 134 us; the launch traced here: 131 us
  Pallas kernels  128 us (96%)
  local copies, waits for them, and re-layouts  2.28 us (2%)
    pallas_call x1, Pallas kernels, shards(): pl.pallas_call(kernel, out_shape=(shape((128, HALF), BF16), shape((128, H...  125 us
    pallas_call x1, Pallas kernels, shards(): pl.pallas_call(finish, out_shape=tuple((shape(a, t) for a, t in copied +...  2.89 us

profile of v6, /device:TPU:0, one launch (start us, length us, event | category | flops | bytes accessed | tf_op | source)
XLA Modules:
  0.0 131.2 jit_solution(9014096675980725342)
XLA Ops:
  0.7 0.0 copy-start
  0.7 0.7 copy-done
  1.4 0.1 pad_dynamic-slice_fusion
  1.4 0.0 copy-start.1
  1.4 0.7 copy-done.1
  2.1 0.1 tile.10
  2.2 0.6 fusion.taps_own
  2.8 0.8 broadcast_in_dim.16.ids
  3.6 124.7 %shard_map.220 = (bf16[128,512]{1,0:T(8,128)(2,1)}, f32[128,512]{1,0:T(8,128)}, bf16[4,64,512]{2,1,0:T(8,128)(2,1)}, bf16[864,512]{1,0:T(8,128)(2,1)}, f32[8,1024]{1,0:T(8,128)}) custom-call(bf16[128,512]{1,0:T(8,128)(2,1)} %x_in.1, bf16[128,512]{1,0:T(8,128)(2,1)} %cot_in.1, s32[264,128]{1,0:T(8,128)} %broadcast_in_dim.16.ids, f32[1,512]{1,0:T(1,128)} %bitcast.21, ...), custom_call_target="tpu_custom_call" | custom-call | tf_op jit(solution)/shard_map/pallas_call | solution.py:822
  128.3 2.9 %shard_map.221 = (bf16[128,512]{1,0:T(8,128)(2,1)}, f32[128,512]{1,0:T(8,128)}, f32[64,512]{1,0:T(8,128)}, f32[64,512]{1,0:T(8,128)}, f32[64,512]{1,0:T(8,128)},...) custom-call(bf16[128,512]{1,0:T(8,128)(2,1)} %get-tuple-element.29.b, ...), custom_call_target="tpu_custom_call" | custom-call | tf_op jit(solution)/shard_map/pallas_call | solution.py:860
  (3 shorter events, 0.0 us)
Async XLA Ops:
  0.7 0.7 copy-start
  1.4 0.7 copy-start.1
